TPU v7x, 768 devices: a whole 4x8x12 slice. The times are simulated.
768 devices in a mesh: slab: 96 (over z_lo, y, core), angle: 8 (over x, z_hi).
Axes of the slice: x: 4, y: 8, z: 12 (z_hi: 2, z_lo: 6; z = z_hi * 6 + z_lo), core: 2. Of those that a mesh axis runs over, the one named last changes fastest.
Arguments:
- volume: float32 [1024, 768, 128], P('angle', 'slab'), may hold values from -6 to 6
- dual: float32 [8, 768, 4096], P('angle', 'slab'), may hold values from -6 to 6
- measured: float32 [8, 768, 4096], P('angle', 'slab'), may hold values from -6 to 6
- tiles: bfloat16 [64, 128, 128], replicated, may hold values from -0.09375 to 0.09375
- lists: int32 [3, 96, 8192], P(None, 'slab', 'angle'), may hold values from 0 to 1023, as said below
- live: int32 [96, 64], P('slab', 'angle'), may hold values from 0 to 128, as said below
- dual_kernel: float32 [2, 3], replicated, may hold values from -1 to 1
- primal_kernel: float32 [2, 3], replicated, may hold values from -1 to 1
Outputs:
- new_volume: float32 [1024, 768, 128], P('angle', 'slab')
- new_dual: float32 [8, 768, 4096], P('angle', 'slab')
Inputs may be any that keep to these rules, and one draw needn't show every extreme that they name: Row 0 of lists: position p of a list lies in segment j = (p % 1024) // 128 and names a voxel block of j*128 to (j+1)*128 - 1. Row 1 names a detector block 0 to 31 of the list's own angle group; row 2 a tile 0 to 63. live[s, g*8 + j] counts the live leading positions of segment j of the list of slab s and angle group g.
All inputs are finite; a program needn't handle non-finite values.
Results may differ from a plain program's by a relative error of at most 0.0015.
Values may be sent and summed in bfloat16 or wider, within the bound.
A program may use at most 32 MiB of HBM per device.

v0:
```python
import math

import jax
import jax.numpy as jnp
from jax import lax
from jax.sharding import PartitionSpec as P


def extended(x, sides, width):
    for axis, dim in sides:
        size, length = (lax.axis_size(axis), x.shape[dim])
        up = [(i, (i + 1) % size) for i in range(size - 1)]
        down = [(j, i) for i, j in up]
        last = lax.slice_in_dim(x, length - width, length, axis=dim)
        first = lax.slice_in_dim(x, 0, width, axis=dim)
        before = lax.ppermute(last, axis, up)
        after = lax.ppermute(first, axis, down)
        x = jnp.concatenate([before, x, after], axis=dim)
    return x


def apply_blocks(
    source,
    pick_idx,
    put_idx,
    tile_idx,
    alive_mask,
    tiles,
    out_rows,
    formula,
    seg_len,
    pick_bases,
    pick_span,
    put_bases,
    put_span,
):
    entry_total = pick_idx.shape[0]
    block_len = math.gcd(seg_len, 64)
    start_acc = jnp.zeros((out_rows,) + source.shape[1:-1] + (tiles.shape[1],), jnp.float32)
    pick_range = jnp.arange(pick_span, dtype=jnp.int32)
    put_range = jnp.arange(put_span, dtype=jnp.int32)
    highest = lax.Precision.HIGHEST

    def one_block(block_num, accum):
        begin_at = block_num * block_len
        seg_num = begin_at // seg_len
        pick_base = pick_bases[seg_num]
        put_base = put_bases[seg_num]
        picks = lax.dynamic_slice_in_dim(pick_idx, begin_at, block_len) - pick_base
        puts = lax.dynamic_slice_in_dim(put_idx, begin_at, block_len) - put_base
        tile_pick = lax.dynamic_slice_in_dim(tile_idx, begin_at, block_len)
        masks = lax.dynamic_slice_in_dim(alive_mask, begin_at, block_len)
        window = lax.dynamic_slice_in_dim(source, pick_base, pick_span, 0)
        pick_hot = (picks[:, None] == pick_range[None, :]).astype(source.dtype)
        taken = jnp.einsum(
            "ep,prv->erv", pick_hot, window, preferred_element_type=jnp.float32
        ).astype(source.dtype)
        tile_set = jnp.take(tiles, tile_pick, axis=0)
        product = jnp.einsum(formula, taken, tile_set, preferred_element_type=jnp.float32)
        put_hot = (put_range[:, None] == puts[None, :]).astype(jnp.float32) * masks[None, :]
        added = jnp.einsum("qe,erx->qrx", put_hot, product, precision=highest)
        current = lax.dynamic_slice_in_dim(accum, put_base, put_span, 0)
        return lax.dynamic_update_slice_in_dim(accum, current + added, put_base, 0)

    return lax.fori_loop(0, entry_total // block_len, one_block, start_acc)


def ramp_filter(signal):
    row_total, det_width = signal.shape
    pa_len = 1 << (det_width.bit_length() - 1) // 2
    qa_len = det_width // pa_len
    highest = lax.Precision.HIGHEST
    two_pi = 2.0 * math.pi
    index_p = jnp.arange(pa_len, dtype=jnp.int32)
    index_q = jnp.arange(qa_len, dtype=jnp.int32)
    angle_p = two_pi * (index_p[:, None] * index_p[None, :] % pa_len).astype(jnp.float32) / pa_len
    angle_q = two_pi * (index_q[:, None] * index_q[None, :] % qa_len).astype(jnp.float32) / qa_len
    angle_t = (
        two_pi * (index_p[:, None] * index_q[None, :] % det_width).astype(jnp.float32) / det_width
    )
    cos_p, sin_p = (jnp.cos(angle_p), jnp.sin(angle_p))
    cos_q, sin_q = (jnp.cos(angle_q), jnp.sin(angle_q))
    cos_t, sin_t = (jnp.cos(angle_t), jnp.sin(angle_t))
    freq = index_p[:, None] + pa_len * index_q[None, :]
    ramp = 2.0 * jnp.minimum(freq, det_width - freq).astype(jnp.float32) / det_width / det_width
    grid = signal.reshape(row_total, pa_len, qa_len)
    a_re = jnp.einsum("mnq,nk->mkq", grid, cos_p, precision=highest)
    a_im = -jnp.einsum("mnq,nk->mkq", grid, sin_p, precision=highest)
    b_re = a_re * cos_t + a_im * sin_t
    b_im = a_im * cos_t - a_re * sin_t
    c_re = jnp.einsum("mkq,qj->mkj", b_re, cos_q, precision=highest) + jnp.einsum(
        "mkq,qj->mkj", b_im, sin_q, precision=highest
    )
    c_im = jnp.einsum("mkq,qj->mkj", b_im, cos_q, precision=highest) - jnp.einsum(
        "mkq,qj->mkj", b_re, sin_q, precision=highest
    )
    y_re = c_re * ramp
    y_im = c_im * ramp
    d_re = jnp.einsum("mkj,jq->mkq", y_re, cos_q, precision=highest) - jnp.einsum(
        "mkj,jq->mkq", y_im, sin_q, precision=highest
    )
    d_im = jnp.einsum("mkj,jq->mkq", y_im, cos_q, precision=highest) + jnp.einsum(
        "mkj,jq->mkq", y_re, sin_q, precision=highest
    )
    e_re = d_re * cos_t - d_im * sin_t
    e_im = d_im * cos_t + d_re * sin_t
    f_re = jnp.einsum("mkq,kn->mnq", e_re, cos_p, precision=highest) - jnp.einsum(
        "mkq,kn->mnq", e_im, sin_p, precision=highest
    )
    return f_re.reshape(row_total, det_width)


def to_blocks(sino, blocks_u):
    ang_count, row_count, det_width = sino.shape
    shaped = sino.reshape(ang_count, row_count, blocks_u, det_width // blocks_u)
    return shaped.transpose(0, 2, 1, 3).reshape(
        ang_count * blocks_u, row_count, det_width // blocks_u
    )


def on_device(volume, dual, measured, tiles, lists, live, dual_kernel, primal_kernel):
    groups = lax.axis_size("angle")
    entry_count = lists.shape[2]
    seg_len = entry_count // groups
    ang_local, row_count, det_width = dual.shape
    vox_local, _rows_unused, blk_width = volume.shape
    blocks_u = det_width // blk_width
    det_blocks = ang_local * blocks_u
    positions = jnp.arange(entry_count, dtype=jnp.int32)
    alive_own = (positions % seg_len < jnp.repeat(live[0], seg_len)).astype(jnp.float32)
    vox_ids = lists[0, 0]
    det_ids = lists[1, 0]
    tile_ids = lists[2, 0]
    seg_numbers = jnp.arange(groups, dtype=jnp.int32)
    zero_bases = jnp.zeros((groups,), jnp.int32)
    gathered = lax.all_gather(volume.astype(jnp.bfloat16), "angle", axis=0, tiled=True)
    projected = apply_blocks(
        gathered,
        vox_ids,
        det_ids,
        tile_ids,
        alive_own,
        tiles,
        det_blocks,
        "erv,edv->erd",
        seg_len,
        seg_numbers * vox_local,
        vox_local,
        zero_bases,
        det_blocks,
    )
    projected = projected.reshape(ang_local, blocks_u, row_count, blk_width).transpose(0, 2, 1, 3)
    misfit = projected.reshape(ang_local, row_count, det_width) - measured
    padded = extended(jnp.stack([dual, misfit]), (("slab", 2),), 1)
    summed = jnp.zeros_like(dual)
    for shift_idx in range(3):
        summed = (
            summed + dual_kernel[0, shift_idx] * padded[0, :, shift_idx : shift_idx + row_count]
        )
        summed = (
            summed + dual_kernel[1, shift_idx] * padded[1, :, shift_idx : shift_idx + row_count]
        )
    new_dual = dual + summed
    filtered = ramp_filter(new_dual.reshape(ang_local * row_count, det_width))
    filtered = filtered.reshape(ang_local, row_count, det_width).astype(jnp.bfloat16)
    q_blocks = to_blocks(filtered, blocks_u)
    row_span = lax.axis_size("angle") * vox_local
    seg_count = row_span // vox_local
    local_segs = jnp.arange(seg_count, dtype=jnp.int32)
    back_own = lax.psum_scatter(
        apply_blocks(
            q_blocks,
            det_ids,
            vox_ids,
            tile_ids,
            alive_own,
            tiles,
            row_span,
            "erd,edv->erv",
            seg_len,
            jnp.zeros((seg_count,), jnp.int32),
            det_blocks,
            local_segs * vox_local,
            vox_local,
        ),
        "angle",
        scatter_dimension=0,
        tiled=True,
    )
    padded_vol = extended(jnp.stack([volume, back_own]), (("slab", 2),), 1)
    summed_vol = jnp.zeros_like(volume)
    for shift_idx in range(3):
        summed_vol = (
            summed_vol
            + primal_kernel[0, shift_idx] * padded_vol[0, :, shift_idx : shift_idx + row_count]
        )
        summed_vol = (
            summed_vol
            + primal_kernel[1, shift_idx] * padded_vol[1, :, shift_idx : shift_idx + row_count]
        )
    new_volume = volume + summed_vol
    return (new_volume, new_dual)


def solution(mesh):
    in_specs = (
        P("angle", "slab", None),
        P("angle", "slab", None),
        P("angle", "slab", None),
        P(),
        P(None, "slab", "angle"),
        P("slab", "angle"),
        P(),
        P(),
    )
    out_specs = (P("angle", "slab", None), P("angle", "slab", None))
    return jax.shard_map(
        on_device, mesh=mesh, in_specs=in_specs, out_specs=out_specs, check_vma=False
    )
```

profile of v0, /device:TPU:1, one launch (start us, length us, event | category | flops | bytes accessed | tf_op | source)
XLA Modules:
  0.0 652.3 jit_solution(14425281970225376530)
XLA Ops:
  10.9 112.7 %all-gather.2.cloned.1.call-done = bf16[1024,8,128]{2,1,0:T(8,128)(2,1)} async-done(((bf16[128,8,128]{2,1,0:T(8,128)(2,1)}), bf16[1024,8,128]{2,1,0:T(8,128)(2,1)}) %all-gather.2.cloned.1.call-update) | async-done | bytes 2097168 | tf_op jit(solution)/shard_map/all_gather | solution.py:136
  123.6 142.4 %while.33 = (s32[]{:T(128)}, f32[32,8,128]{2,0,1:T(8,128)S(1)}, s32[1024]{0:T(1024)S(1)}, f32[1024]{0:T(1024)S(1)}, s32[1024]{0:T(1024)S(1)}, /*index=5*/s32[8]{...) while((s32[]{:T(128)}, f32[32,8,128]{2,0,1:T(8,128)S(1)}, ...), condition=%wide.region_1.3_spmd.clone, body=%wide.region_0.2_spmd.clone.sunk | while | flops 59848152 | bytes 8134474 | solution.py:65
  128.2 2.5 gather_fusion.1
  137.1 2.5 gather_fusion.1
  146.0 2.5 gather_fusion.1
  154.9 2.5 gather_fusion.1
  163.8 2.5 gather_fusion.1
  172.7 2.5 gather_fusion.1
  181.6 2.5 gather_fusion.1
  190.5 2.5 gather_fusion.1
  199.4 2.5 gather_fusion.1
  208.3 2.5 gather_fusion.1
  217.2 2.5 gather_fusion.1
  226.1 2.5 gather_fusion.1
  235.0 2.5 gather_fusion.1
  243.9 2.5 gather_fusion.1
  252.8 2.5 gather_fusion.1
  266.1 5.0 collective-permute-start
  276.3 4.0 fusion.73
  289.2 173.3 %while.32 = (s32[]{:T(128)}, f32[1024,8,128]{2,1,0:T(8,128)}, s32[8]{0:T(128)S(1)}, s32[1024]{0:T(1024)S(1)}, f32[1024]{0:T(1024)S(1)}, /*index=5*/s32[1024]{0:T...) while((s32[]{:T(128)}, f32[1024,8,128]{2,1,0:T(8,128)}, ...), condition=%wide.region_3.5_spmd.clone, body=%wide.region_2.4_spmd.clone.sunk | while | flops 122834392 | bytes 10297156 | solution.py:65
  462.5 163.6 %reduce-scatter.2.cloned.1.call-done = f32[128,8,128]{2,1,0:T(8,128)} async-done(((f32[1024,8,128]{2,1,0:T(8,128)}), f32[128,8,128]{2,1,0:T(8,128)}) %reduce-scatter.2.cloned.1.call-update) | async-done | bytes 524304 | tf_op jit(solution)/shard_map/reduce_scatter | solution.py:170
  627.5 4.9 collective-permute-start.2
  635.1 3.7 collective-permute-done.3
  638.7 6.7 %fusion.49 = f32[128,8,128]{2,1,0:T(8,128)} fusion(f32[128,8,128]{2,1,0:T(8,128)S(1)} %copy-done.1, f32[2,128,1,128]{3,2,1,0:T(1,128)S(1)} %collective-permute-done.3, f32[1,128,8,128]{3,2,1,0:T(8,128)} %bitcast.157, f32[1,128,8,128]{3,2,1,0:T(8,128)S(1)} %bitcast.154, f32[2,128,1,128]{3,2,1,0:T(1,128)S(1)} %collective-permute-done.2, ...), kind=kLoop, calls=%fused_computation.71 | loop fusion | flops 2621440 | bytes 2883608 | tf_op jit(solution)/shard_map/add | solution.py:201
  (410 shorter events, 239.4 us)
Async XLA Ops:
  7.2 116.4 %all-gather.2.cloned.1.call-start = ((), (), s32[]{:S(2)}) async-start(), calls=%async_computation.1 | async-start | bytes 2359296 | tf_op jit(solution)/shard_map/all_gather | solution.py:136
  9.0 617.1 %reduce-scatter.2.cloned.1.call-start = ((), (), s32[]{:S(2)}) async-start(), calls=%async_computation.2 | async-start | bytes 4718592 | tf_op jit(solution)/shard_map/reduce_scatter | solution.py:170
  123.6 142.4 %copy-start.3 = (f32[1,8,4096]{2,1,0:T(8,128)S(1)}, f32[1,8,4096]{2,1,0:T(8,128)}, u32[]{:S(2)}) copy-start(f32[1,8,4096]{2,1,0:T(8,128)} %param.16) | copy-start | bytes 393220
  123.6 142.5 %copy-start.2 = (f32[1,8,4096]{2,1,0:T(8,128)S(1)}, f32[1,8,4096]{2,1,0:T(8,128)}, u32[]{:S(2)}) copy-start(f32[1,8,4096]{2,1,0:T(8,128)} %param.15) | copy-start | bytes 393220
  123.6 149.4 %copy-start.5 = (f32[2,3]{1,0:T(2,128)S(1)}, f32[2,3]{1,0:T(2,128)}, u32[]{:S(2)}) copy-start(f32[2,3]{1,0:T(2,128)} %param.20) | copy-start | bytes 76
  266.1 7.8 %collective-permute-start = (f32[2,1,1,4096]{3,2,1,0:T(1,128)S(1)}, f32[2,1,1,4096]{3,2,1,0:T(1,128)S(1)}, u32[]{:S(2)}, u32[]{:S(2)}) collective-permute-start(f32[2,1,1,4096]{3,2,1,0:T(1,128)S(1)} %get-tuple-element.632), channel_id=1, source_target_pairs={{0,8},{8,16},{16,24},{24,32},{32,40},{40,48},{48,56},{56,64},{64,7... | collective-permute-start | bytes 98312 | tf_op jit(solution)/shard_map/ppermute | solution.py:16
  271.1 5.2 collective-permute-start.1
  280.3 2.7 copy-start.4
  286.7 2.4 copy-start
  462.5 163.7 %copy-start.1 = (f32[128,8,128]{2,1,0:T(8,128)S(1)}, f32[128,8,128]{2,1,0:T(8,128)}, u32[]{:S(2)}) copy-start(f32[128,8,128]{2,1,0:T(8,128)} %param.14) | copy-start | bytes 1572868
  462.5 171.9 %copy-start.6 = (f32[2,3]{1,0:T(2,128)S(1)}, f32[2,3]{1,0:T(2,128)}, u32[]{:S(2)}) copy-start(f32[2,3]{1,0:T(2,128)} %param.21) | copy-start | bytes 76
  627.5 7.6 %collective-permute-start.2 = (f32[2,128,1,128]{3,2,1,0:T(1,128)S(1)}, f32[2,128,1,128]{3,2,1,0:T(1,128)S(1)}, u32[]{:S(2)}, u32[]{:S(2)}) collective-permute-start(f32[2,128,1,128]{3,2,1,0:T(1,128)S(1)} %get-tuple-element.630), channel_id=1, source_target_pairs={{0,8},{8,16},{16,24},{24,32},{32,40},{40,48},{48,56},{56,64},{64,7... | collective-permute-start | bytes 393224 | tf_op jit(solution)/shard_map/ppermute | solution.py:16
  632.4 6.3 collective-permute-start.3
Sparse Core Ops, SparseCore 0:
  12.4 111.1 all-gather.1
  462.6 163.4 reduce-scatter.1
where the time goes:
time: 657 us; the launch traced here: 652 us
  waiting for transfers between devices  282 us (43%)
  local copies, waits for them, and re-layouts  154 us (23%)
  matrix products  88.1 us (13%)
  loops' own time  59.8 us (9%)
  other arithmetic  39.5 us (6%)
  between operations  14.3 us (2%)
  starting transfers between devices  13.8 us (2%)
    reduce_scatter x1, waiting for transfers between devices, on_device(): lax.psum_scatter(apply_blocks(q_blocks, det_ids, vox_ids, tile_ids, alive...  164 us
    all_gather x1, waiting for transfers between devices, on_device(): lax.all_gather(volume.astype(jnp.bfloat16), 'angle', axis=0, tiled=True)  113 us
    gather x32, local copies, waits for them, and re-layouts, one_block(): tile_set = jnp.take(tiles, tile_pick, axis=0)  75.2 us
    another operation x2, loops' own time, apply_blocks(): return lax.fori_loop(0, entry_total // block_len, one_block, start_acc)  59.8 us
    dot_general x32, matrix products, one_block(): jnp.einsum(formula, taken, tile_set, preferred_element_type=jnp.float32)  56.8 us
    dot_general x32, matrix products, one_block(): added = jnp.einsum('qe,erx->qrx', put_hot, product, precision=highest)  17.8 us
    dynamic_update_slice x16, local copies, waits for them, and re-layouts, one_block(): return lax.dynamic_update_slice_in_dim(accum, current + added, put_base, 0)  17.7 us
    dynamic_slice x16, local copies, waits for them, and re-layouts, one_block(): current = lax.dynamic_slice_in_dim(accum, put_base, put_span, 0)  17.3 us
  transfers between devices with their start and end apart: 6, of which 4 were waited for; matrix products, arithmetic and copies ran while one was open for 1% of the time, Pallas kernels for 0%

commit v1 on v0

v1 whole, which is shorter than its diff:
```python
import functools

import jax
import jax.numpy as jnp
import ml_dtypes
import numpy as np
from jax import lax
from jax.experimental import pallas as pl
from jax.experimental.pallas import tpu as pltpu
from jax.sharding import PartitionSpec as P

F32 = jnp.float32
BF16 = jnp.bfloat16
MESH = pl.DeviceIdType.MESH
CONTRACT_LAST = (((1,), (1,)), ((), ()))
CONTRACT_INNER = (((1,), (0,)), ((), ()))
VMEM_LIMIT = 56 * 2**20
X_SIZE = 4
CHUNKS = 4


def ramp_matrix(width, blk):
    n = np.arange(width)
    taps = np.zeros(width)
    odd = n % 2 == 1
    taps[odd] = -(2.0 / width**2) / np.sin(np.pi * n[odd] / width) ** 2
    k = np.arange(width // blk)[:, None, None]
    i = np.arange(blk)[None, :, None]
    j = np.arange(blk)[None, None, :]
    full = taps[(blk * k + j - i) % width].reshape(width, blk)
    high = full.astype(ml_dtypes.bfloat16)
    low = (full - high.astype(np.float64)).astype(ml_dtypes.bfloat16)
    return np.concatenate([high, low], axis=1)


def greet(partners, conditional):
    barrier = pltpu.get_barrier_semaphore()
    for partner in partners:
        pl.semaphore_signal(barrier, inc=1, device_id=partner, device_id_type=MESH)
    for present, partner in conditional:

        @pl.when(present)
        def _():
            pl.semaphore_signal(barrier, inc=1, device_id=partner, device_id_type=MESH)

    present_count = sum([present.astype(jnp.int32) for present, _partner in conditional], jnp.int32(len(partners)))
    pl.semaphore_wait(barrier, present_count)


def remote(src, dst, send, recv, device):
    return pltpu.make_async_remote_copy(
        src_ref=src, dst_ref=dst, send_sem=send, recv_sem=recv, device_id=device, device_id_type=MESH
    )


def lists_kernel(groups, in_ref, out_ref, land, send, recv):
    slab, me = lax.axis_index("slab"), lax.axis_index("angle")
    greet([(slab, lax.rem(me + d, groups)) for d in range(1, groups)], [])
    copies = []
    for d in range(1, groups):
        to = lax.rem(me + d, groups)
        copy = remote(in_ref.at[to], land.at[me], send.at[d - 1], recv.at[d - 1], (slab, to))
        copy.start()
        copies.append(copy)
    land[me] = in_ref[me]
    for copy in copies:
        copy.wait()
    out_ref[...] = land[...]


def forward_kernel(idx_ref, vol_ref, tiles_ref, out_ref, dense, rounded, *sums):
    blocks = vol_ref.shape[0]
    groups, rows, blk = out_ref.shape
    tile_count = tiles_ref.shape[0]
    rounded[...] = vol_ref[...].reshape(blocks * 8, blk).astype(BF16)
    for total in sums:
        total[...] = jnp.zeros_like(total)

    def products(i, _):
        pair = tiles_ref[pl.ds(i * 2, 2)].reshape(2 * blk, blk)
        both = lax.dot_general(rounded[...], pair, CONTRACT_LAST, preferred_element_type=F32)
        dense[pl.ds(i * 2 * blocks, blocks)] = both[:, :blk].reshape(blocks, 8, blk)
        dense[pl.ds((i * 2 + 1) * blocks, blocks)] = both[:, blk:].reshape(blocks, 8, blk)
        return 0

    lax.fori_loop(0, tile_count // 2, products, 0)

    def add(i, _):
        for u in range(4):
            for g in range(groups):
                p = i * 4 + u
                sums[g][idx_ref[g, 1, p]] += dense[idx_ref[g, 2, p] * blocks + idx_ref[g, 0, p]]
        return 0

    lax.fori_loop(0, idx_ref.shape[2] // 4, add, 0)
    for g in range(groups):
        out_ref[g] = sums[g][: rows // 8].reshape(rows, blk).astype(BF16)


def backward_kernel(idx_ref, q_ref, tiles_ref, out_ref, wide, spread):
    blocks = out_ref.shape[0]
    groups, rows, blk = q_ref.shape
    det = rows // 8
    tile_count = tiles_ref.shape[0]
    for g in range(groups):
        wide[pl.ds(g * (det + 1), det)] = q_ref[g].reshape(det, 8, blk).astype(F32)
        wide[g * (det + 1) + det] = jnp.zeros((8, blk), F32)

    def clear(i, _):
        spread[pl.ds(i * blocks, blocks)] = jnp.zeros((blocks, 8, blk), F32)
        return 0

    lax.fori_loop(0, tile_count, clear, 0)

    def add(i, _):
        for u in range(2):
            for g in range(groups):
                p = i * 2 + u
                source = wide[idx_ref[g, 1, p] + g * (det + 1)]
                spread[idx_ref[g, 2, p] * blocks + idx_ref[g, 0, p]] += source
        return 0

    lax.fori_loop(0, idx_ref.shape[2] // 2, add, 0)
    out_ref[...] = jnp.zeros_like(out_ref)

    def products(i, _):
        left = spread[pl.ds(i * 2 * blocks, blocks)].reshape(blocks * 8, blk).astype(BF16)
        right = spread[pl.ds((i * 2 + 1) * blocks, blocks)].reshape(blocks * 8, blk).astype(BF16)
        both = jnp.concatenate([left, right], axis=1)
        pair = tiles_ref[pl.ds(i * 2, 2)].reshape(2 * blk, blk)
        added = lax.dot_general(both, pair, CONTRACT_INNER, preferred_element_type=F32)
        out_ref[...] += added.reshape(blocks, 8, blk)
        return 0

    lax.fori_loop(0, tile_count // 2, products, 0)


def dual_kernel_body(
    slabs,
    part_ref,
    dual_ref,
    meas_ref,
    ramp_ref,
    weights,
    new_ref,
    q_ref,
    land_x,
    send_z,
    land_z,
    own,
    misfit,
    down,
    up,
    from_prev,
    from_next,
    even,
    odd,
    even_low,
    odd_low,
    sx,
    rx,
    sz,
    rz,
    se,
    re,
    gx_s,
    gx_r,
    gz_s,
    gz_r,
    fx_s,
    fx_r,
):
    slab, me = lax.axis_index("slab"), lax.axis_index("angle")
    x, z = me // 2, lax.rem(me, 2)
    partner = (slab, 2 * x + 1 - z)
    has_prev, has_next = slab > 0, slab < slabs - 1
    prev, following = (slab - 1, me), (slab + 1, me)
    peers = [lax.rem(x + d, X_SIZE) for d in range(1, X_SIZE)]
    rows, blk = part_ref.shape[1:]
    width = dual_ref.shape[1]
    det = width // blk
    greet([(slab, 2 * t + z) for t in peers] + [partner], [(has_prev, prev), (has_next, following)])

    step = rows // CHUNKS
    x_copies = []
    for c in range(CHUNKS):
        part = pl.ds(c * step, step)
        line = []
        for d, t in enumerate(peers):
            copy = remote(
                part_ref.at[pl.ds(2 * t, 2), part], land_x.at[d, :, part], sx.at[d, c], rx.at[d, c], (slab, 2 * t + z)
            )
            copy.start()
            line.append(copy)
        x_copies.append(line)
    z_copies = []
    for c in range(CHUNKS):
        part = pl.ds(c * step, step)
        for copy in x_copies[c]:
            copy.wait_recv()
        for side in (1, 0):
            k = 1 - z if side else z
            total = part_ref[2 * x + k, part].astype(F32)
            for d in range(X_SIZE - 1):
                total = total + land_x[d, k, part].astype(F32)
            if side:
                send_z[part] = total.astype(BF16)
                copy = remote(send_z.at[part], land_z.at[part], sz.at[c], rz.at[c], partner)
                copy.start()
                z_copies.append(copy)
            else:
                own[part] = total
    for c in range(CHUNKS):
        z_copies[c].wait_recv()
        for b in range(c * step // 8, (c + 1) * step // 8, 2):
            both = own[pl.ds(b * 8, 16)] + land_z[pl.ds(b * 8, 16)].astype(F32)
            cols = pl.ds(b * blk, blk)
            misfit[:, cols] = both[:8] - meas_ref[:, cols]
            cols = pl.ds((b + 1) * blk, blk)
            misfit[:, cols] = both[8:] - meas_ref[:, cols]

    down[...] = weights[0, 0] * dual_ref[7:8, :] + weights[1, 0] * misfit[7:8, :]
    up[...] = weights[0, 2] * dual_ref[0:1, :] + weights[1, 2] * misfit[0:1, :]
    to_next = remote(down, from_prev, se.at[0], re.at[0], following)
    to_prev = remote(up, from_next, se.at[1], re.at[1], prev)

    @pl.when(has_next)
    def _():
        to_next.start()

    @pl.when(has_prev)
    def _():
        to_prev.start()

    @pl.when(has_prev)
    def _():
        to_next.wait_recv()

    @pl.when(jnp.logical_not(has_prev))
    def _():
        from_prev[...] = jnp.zeros_like(from_prev)

    @pl.when(has_next)
    def _():
        to_prev.wait_recv()

    @pl.when(jnp.logical_not(has_next))
    def _():
        from_next[...] = jnp.zeros_like(from_next)

    row = lax.broadcasted_iota(jnp.int32, (8, blk), 0)

    def updated(b):
        cols = pl.ds(b * blk, blk)
        dual, mis = dual_ref[:, cols], misfit[:, cols]
        before = pltpu.roll(weights[0, 0] * dual + weights[1, 0] * mis, 1, 0)
        after = pltpu.roll(weights[0, 2] * dual + weights[1, 2] * mis, 7, 0)
        before = jnp.where(row == 0, from_prev[:, cols], before)
        after = jnp.where(row == 7, from_next[:, cols], after)
        new = dual + weights[0, 1] * dual + weights[1, 1] * mis + before + after
        new_ref[:, cols] = new
        return new

    def split(value):
        high = value.astype(BF16)
        return high, (value - high.astype(F32)).astype(BF16)

    news = [updated(b) for b in range(det)]
    for b in range(det):
        high, low = split(jnp.concatenate([news[b], news[(b + 1) % det]], axis=0))
        if b % 2 == 0:
            for base in (0, rows):
                even[pl.ds(base + b * 8, 16)] = high
                even_low[pl.ds(base + b * 8, 16)] = low
        else:
            for base in (0, rows):
                odd[pl.ds(base + (b - 1) * 8, 16)] = high
                odd_low[pl.ds(base + (b - 1) * 8, 16)] = low
    total = jnp.zeros((rows, 2 * blk), F32)
    small = jnp.zeros((rows, blk), F32)
    for k in range(0, det, 2):
        first = pl.ds((det - k) * 8 % rows, rows)
        second = pl.ds((det - k - 2) * 8, rows)
        weight = ramp_ref[pl.ds(k * blk, 2 * blk)]
        high = jnp.concatenate([even[first], odd[second]], axis=1)
        low = jnp.concatenate([even_low[first], odd_low[second]], axis=1)
        total = total + lax.dot_general(high, weight, CONTRACT_INNER, preferred_element_type=F32)
        small = small + lax.dot_general(low, weight[:, :blk], CONTRACT_INNER, preferred_element_type=F32)
    small = small + total[:, blk:] + total[:, :blk]
    for b in range(0, det, 2):
        pair = jnp.concatenate([new_ref[:, pl.ds(b * blk, blk)], new_ref[:, pl.ds((b + 1) * blk, blk)]], axis=0)
        q_ref[me, pl.ds(b * 8, 16)] = (0.5 * pair + small[b * 8 : b * 8 + 16]).astype(BF16)

    halves = 2
    step = rows // halves
    across, around, onward = [], [], []
    for c in range(halves):
        mine = q_ref.at[me, pl.ds(c * step, step)]
        copy = remote(mine, mine, gz_s.at[c], gz_r.at[c], partner)
        copy.start()
        across.append(copy)
    for d, t in enumerate(peers):
        copy = remote(q_ref.at[me], q_ref.at[me], gx_s.at[d], gx_r.at[d], (slab, 2 * t + z))
        copy.start()
        around.append(copy)
    for c in range(halves):
        across[c].wait_recv()
        theirs = q_ref.at[2 * x + 1 - z, pl.ds(c * step, step)]
        for d, t in enumerate(peers):
            copy = remote(theirs, theirs, fx_s.at[d, c], fx_r.at[d, c], (slab, 2 * t + z))
            copy.start()
            onward.append(copy)
    for copy in around + onward:
        copy.wait_recv()
    for line in x_copies:
        for copy in line:
            copy.wait_send()
    for copy in z_copies + across + around + onward:
        copy.wait_send()

    @pl.when(has_next)
    def _():
        to_next.wait_send()

    @pl.when(has_prev)
    def _():
        to_prev.wait_send()


def primal_kernel_body(
    slabs, vol_ref, back_ref, weights, new_ref, down, up, from_prev, from_next, send, recv
):
    slab, me = lax.axis_index("slab"), lax.axis_index("angle")
    has_prev, has_next = slab > 0, slab < slabs - 1
    prev, following = (slab - 1, me), (slab + 1, me)
    greet([], [(has_prev, prev), (has_next, following)])
    down[...] = weights[0, 0] * vol_ref[:, 7, :] + weights[1, 0] * back_ref[:, 7, :]
    up[...] = weights[0, 2] * vol_ref[:, 0, :] + weights[1, 2] * back_ref[:, 0, :]
    to_next = remote(down, from_prev, send.at[0], recv.at[0], following)
    to_prev = remote(up, from_next, send.at[1], recv.at[1], prev)

    @pl.when(has_next)
    def _():
        to_next.start()

    @pl.when(has_prev)
    def _():
        to_prev.start()

    row = lax.broadcasted_iota(jnp.int32, (1, 8, vol_ref.shape[2]), 1)

    def one(i, _):
        here = pl.ds(i * 8, 8)
        vol, back = vol_ref[here], back_ref[here]
        before = pltpu.roll(weights[0, 0] * vol + weights[1, 0] * back, 1, 1)
        after = pltpu.roll(weights[0, 2] * vol + weights[1, 2] * back, 7, 1)
        before = jnp.where(row == 0, 0.0, before)
        after = jnp.where(row == 7, 0.0, after)
        new_ref[here] = vol + weights[0, 1] * vol + weights[1, 1] * back + before + after
        return 0

    lax.fori_loop(0, vol_ref.shape[0] // 8, one, 0)

    @pl.when(has_prev)
    def _():
        to_next.wait_recv()
        new_ref[:, 0, :] += from_prev[...]

    @pl.when(has_next)
    def _():
        to_prev.wait_recv()
        new_ref[:, 7, :] += from_next[...]

    @pl.when(has_next)
    def _():
        to_next.wait_send()

    @pl.when(has_prev)
    def _():
        to_prev.wait_send()


def on_device(volume, dual, measured, tiles, lists, live, dual_kernel, primal_kernel):
    groups, slabs = lax.axis_size("angle"), lax.axis_size("slab")
    seg = lists.shape[2] // groups
    blocks, _, blk = volume.shape
    width = dual.shape[2]
    det = width // blk
    rows = det * 8
    vmem, smem = pl.BlockSpec(memory_space=pltpu.VMEM), pl.BlockSpec(memory_space=pltpu.SMEM)
    dma = pltpu.SemaphoreType.DMA

    parts = lists[:, 0].reshape(3, groups, seg)
    alive = jnp.arange(seg, dtype=jnp.int32)[None, :] < live[0][:, None]
    vox = parts[0] - jnp.arange(groups, dtype=jnp.int32)[:, None] * blocks
    rows_of = jnp.stack([vox, jnp.where(alive, parts[1], det), parts[2]], axis=1)
    rows_of = jnp.pad(rows_of, ((0, 0), (0, 5), (0, 0)))
    index = pl.pallas_call(
        functools.partial(lists_kernel, groups),
        out_shape=jax.ShapeDtypeStruct(rows_of.shape, jnp.int32),
        in_specs=[vmem],
        out_specs=vmem,
        scratch_shapes=[pltpu.VMEM(rows_of.shape, jnp.int32), dma((groups - 1,)), dma((groups - 1,))],
        compiler_params=pltpu.CompilerParams(collective_id=0, has_side_effects=True),
    )(rows_of)

    partial = pl.pallas_call(
        forward_kernel,
        out_shape=jax.ShapeDtypeStruct((groups, rows, blk), BF16),
        in_specs=[smem, vmem, vmem],
        out_specs=vmem,
        scratch_shapes=[
            pltpu.VMEM((tiles.shape[0] * blocks, 8, blk), F32),
            pltpu.VMEM((blocks * 8, blk), BF16),
        ]
        + [pltpu.VMEM((det + 1, 8, blk), F32)] * groups,
        compiler_params=pltpu.CompilerParams(vmem_limit_bytes=VMEM_LIMIT),
    )(index, volume, tiles)

    new_dual, filtered = pl.pallas_call(
        functools.partial(dual_kernel_body, slabs),
        out_shape=[
            jax.ShapeDtypeStruct((8, width), F32),
            jax.ShapeDtypeStruct((groups, rows, blk), BF16),
        ],
        in_specs=[vmem, vmem, vmem, vmem, smem],
        out_specs=[vmem, vmem],
        scratch_shapes=[
            pltpu.VMEM((X_SIZE - 1, 2, rows, blk), BF16),
            pltpu.VMEM((rows, blk), BF16),
            pltpu.VMEM((rows, blk), BF16),
            pltpu.VMEM((rows, blk), F32),
            pltpu.VMEM((8, width), F32),
        ]
        + [pltpu.VMEM((1, width), F32)] * 4
        + [pltpu.VMEM((2 * rows, blk), BF16)] * 4
        + [dma((X_SIZE - 1, CHUNKS))] * 2
        + [dma((CHUNKS,))] * 2
        + [dma((2,))] * 2
        + [dma((X_SIZE - 1,))] * 2
        + [dma((2,))] * 2
        + [dma((X_SIZE - 1, 2))] * 2,
        compiler_params=pltpu.CompilerParams(
            collective_id=1, has_side_effects=True, vmem_limit_bytes=VMEM_LIMIT
        ),
    )(partial, dual[0], measured[0], jnp.asarray(ramp_matrix(width, blk)), dual_kernel)

    back = pl.pallas_call(
        backward_kernel,
        out_shape=jax.ShapeDtypeStruct((blocks, 8, blk), F32),
        in_specs=[smem, vmem, vmem],
        out_specs=vmem,
        scratch_shapes=[
            pltpu.VMEM((groups * (det + 1), 8, blk), F32),
            pltpu.VMEM((tiles.shape[0] * blocks, 8, blk), F32),
        ],
        compiler_params=pltpu.CompilerParams(vmem_limit_bytes=VMEM_LIMIT),
    )(index, filtered, tiles)

    new_volume = pl.pallas_call(
        functools.partial(primal_kernel_body, slabs),
        out_shape=jax.ShapeDtypeStruct(volume.shape, F32),
        in_specs=[vmem, vmem, smem],
        out_specs=vmem,
        scratch_shapes=[pltpu.VMEM((blocks, blk), F32)] * 4 + [dma((2,))] * 2,
        compiler_params=pltpu.CompilerParams(
            collective_id=2, has_side_effects=True, vmem_limit_bytes=VMEM_LIMIT
        ),
    )(volume, back, primal_kernel)
    return (new_volume, new_dual[None])


def solution(mesh):
    in_specs = (
        P("angle", "slab", None),
        P("angle", "slab", None),
        P("angle", "slab", None),
        P(),
        P(None, "slab", "angle"),
        P("slab", "angle"),
        P(),
        P(),
    )
    out_specs = (P("angle", "slab", None), P("angle", "slab", None))
    return jax.shard_map(
        on_device, mesh=mesh, in_specs=in_specs, out_specs=out_specs, check_vma=False
    )
```

time: 657 us -> 111 us (0.17)
  waiting for transfers between devices: 282 us -> 0 us
  local copies, waits for them, and re-layouts: 154 us -> 3.84 us
  Pallas kernels: 0 us -> 104 us
  matrix products: 88.1 us -> 0 us
  loops' own time: 59.8 us -> 0 us
  other arithmetic: 39.5 us -> 0.8 us
  starting transfers between devices: 13.8 us -> 0 us
  between operations: 14.3 us -> 0.68 us
    reduce_scatter x1 -> x0, waiting for transfers between devices: 164 us -> none  [on_device(): lax.psum_scatter(apply_blocks(q_blocks, det_ids, vox_ids, tile_ids, alive...]
    all_gather x1 -> x0, waiting for transfers between devices: 113 us -> none  [on_device(): lax.all_gather(volume.astype(jnp.bfloat16), 'angle', axis=0, tiled=True)]
    pallas_call x0 -> x5, Pallas kernels: none -> 104 us  [the longest x1 39.2 us: on_device(): pl.pallas_call(functools.partial(dual_kernel_body, slabs), out_shape=[jax...]
    dot_general x108 -> x0, matrix products: 88.1 us -> none  [the longest x32 56.8 us: one_block(): jnp.einsum(formula, taken, tile_set, preferred_element_type=jnp.float32)]
    gather x32 -> x0, local copies, waits for them, and re-layouts: 75.2 us -> none  [one_block(): tile_set = jnp.take(tiles, tile_pick, axis=0)]
    another operation x2 -> x0, loops' own time: 59.8 us -> none  [apply_blocks(): return lax.fori_loop(0, entry_total // block_len, one_block, start_acc)]
    dynamic_slice x128 -> x0, local copies, waits for them, and re-layouts: 56.5 us -> none  [the longest x16 17.3 us: one_block(): current = lax.dynamic_slice_in_dim(accum, put_base, put_span, 0)]
    sub x32 -> x1, other arithmetic: 21.8 us -> 0.78 us  [on_device(): vox = parts[0] - jnp.arange(groups, dtype=jnp.int32)[:, None] * blocks]
  transfers between devices with their start and end apart: 6 -> 0, of which waited for: 4 -> 0; matrix products, arithmetic and copies ran while one was open for 1% -> 0% of each run, Pallas kernels for 0% -> 0%
where the time goes in v1:
time: 111 us; the launch traced here: 109 us
  Pallas kernels  104 us (94%)
  local copies, waits for them, and re-layouts  3.84 us (3%)
    pallas_call x1, Pallas kernels, on_device(): pl.pallas_call(functools.partial(dual_kernel_body, slabs), out_shape=[jax...  39.2 us
    pallas_call x1, Pallas kernels, on_device(): pl.pallas_call(functools.partial(lists_kernel, groups), out_shape=jax.Sha...  20.8 us
    pallas_call x1, Pallas kernels, on_device(): pl.pallas_call(backward_kernel, out_shape=jax.ShapeDtypeStruct((blocks, 8...  20.4 us
    pallas_call x1, Pallas kernels, on_device(): pl.pallas_call(forward_kernel, out_shape=jax.ShapeDtypeStruct((groups, ro...  16.5 us
    pallas_call x1, Pallas kernels, on_device(): pl.pallas_call(functools.partial(primal_kernel_body, slabs), out_shape=ja...  7.07 us
    unnamed x4, local copies, waits for them, and re-layouts  2.53 us

profile of v1, /device:TPU:1, one launch (start us, length us, event | category | flops | bytes accessed | tf_op | source)
XLA Modules:
  0.0 109.3 jit_solution(13031157223872070610)
XLA Ops:
  0.6 0.7 slice_bitcast_fusion
  1.3 0.8 bitcast_subtract_fusion
  2.1 0.6 pad.4.in_ref
  2.8 20.8 %shard_map.104.idx_ref = s32[8,8,128]{2,1,0:T(8,128)} custom-call(s32[8,8,128]{2,1,0:T(8,128)} %pad.4.in_ref), custom_call_target="tpu_custom_call" | custom-call | tf_op jit(solution)/shard_map/pallas_call | solution.py:398
  23.6 16.5 %shard_map.105.part_ref = bf16[8,256,128]{2,1,0:T(8,128)(2,1)} custom-call(s32[8,8,128]{2,1,0:T(8,128)} %shard_map.104.idx_ref, f32[128,8,128]{2,1,0:T(8,128)} %vol_ref.3, bf16[64,128,128]{2,1,0:T(8,128)(2,1)} %tiles_ref.3), custom_call_target="tpu_custom_call" | custom-call | tf_op jit(solution)/shard_map/pallas_call | solution.py:407
  40.1 39.2 %shard_map.106 = (f32[8,4096]{1,0:T(8,128)}, bf16[8,256,128]{2,1,0:T(8,128)(2,1)}) custom-call(bf16[8,256,128]{2,1,0:T(8,128)(2,1)} %shard_map.105.part_ref, f32[8,4096]{1,0:T(8,128)} %bitcast.11, f32[8,4096]{1,0:T(8,128)} %bitcast.12, bf16[4096,256]{1,0:T(8,128)(2,1)} %constant.8.clone.ramp_ref, f32[2,3]{1,0:T(2,128)} %weights.2), custom_call_target="tpu_custom_call" | custom-call | tf_op jit(solution)/shard_map/pallas_call | solution.py:420
  79.3 20.4 %shard_map.107.back_ref = f32[128,8,128]{2,1,0:T(8,128)} custom-call(s32[8,8,128]{2,1,0:T(8,128)} %shard_map.104.idx_ref, bf16[8,256,128]{2,1,0:T(8,128)(2,1)} %get-tuple-element.4.q_ref, bf16[64,128,128]{2,1,0:T(8,128)(2,1)} %tiles_ref.3), custom_call_target="tpu_custom_call" | custom-call | tf_op jit(solution)/shard_map/pallas_call | solution.py:448
  99.7 0.0 copy-start
  99.7 7.1 %shard_map.108 = f32[128,8,128]{2,1,0:T(8,128)} custom-call(f32[128,8,128]{2,1,0:T(8,128)} %vol_ref.3, f32[128,8,128]{2,1,0:T(8,128)} %shard_map.107.back_ref, f32[2,3]{1,0:T(2,128)} %weights.3), custom_call_target="tpu_custom_call" | custom-call | tf_op jit(solution)/shard_map/pallas_call | solution.py:460
  106.8 1.9 %copy.13 = f32[128,8,128]{2,1,0:T(8,128)} copy(f32[128,8,128]{2,1,0:T(8,128)} %shard_map.108) | data formatting | bytes 1048576
  108.6 0.0 copy-done
  108.6 0.7 copy.14
  (2 shorter events, 0.0 us)
Async XLA Ops:
  99.7 8.9 %copy-start = (f32[8,4096]{1,0:T(8,128)S(1)}, f32[8,4096]{1,0:T(8,128)}, u32[]{:S(2)}) copy-start(f32[8,4096]{1,0:T(8,128)} %get-tuple-element.5) | copy-start | bytes 393220

commit v2 on v0

v2 whole, which is shorter than its diff:
```python
import functools

import jax
import jax.numpy as jnp
import ml_dtypes
import numpy as np
from jax import lax
from jax.experimental import pallas as pl
from jax.experimental.pallas import tpu as pltpu
from jax.sharding import PartitionSpec as P

F32 = jnp.float32
BF16 = jnp.bfloat16
MESH = pl.DeviceIdType.MESH
CONTRACT_LAST = (((1,), (1,)), ((), ()))
CONTRACT_INNER = (((1,), (0,)), ((), ()))
VMEM_LIMIT = 56 * 2**20
X_SIZE = 4


def ramp_matrix(width, blk):
    n = np.arange(width)
    taps = np.zeros(width)
    odd = n % 2 == 1
    taps[odd] = -(2.0 / width**2) / np.sin(np.pi * n[odd] / width) ** 2
    k = np.arange(width // blk)[:, None, None]
    i = np.arange(blk)[None, :, None]
    j = np.arange(blk)[None, None, :]
    full = taps[(blk * k + j - i) % width].reshape(width, blk)
    high = full.astype(ml_dtypes.bfloat16)
    low = (full - high.astype(np.float64)).astype(ml_dtypes.bfloat16)
    return np.concatenate([high, low], axis=1)


def remote(src, dst, send, recv, device):
    return pltpu.make_async_remote_copy(
        src_ref=src, dst_ref=dst, send_sem=send, recv_sem=recv, device_id=device, device_id_type=MESH
    )


def step_kernel(
    slabs,
    lists_ref,
    live_ref,
    vol_ref,
    dual_ref,
    meas_ref,
    tiles_hbm,
    ramp_hbm,
    dual_w,
    primal_w,
    new_vol,
    new_dual,
    tiles,
    ramp,
    dense,
    rounded,
    out_lists,
    in_lists,
    index,
    picked,
    part,
    land_near,
    land_far,
    near,
    send_z,
    land_z,
    misfit,
    down,
    up,
    from_prev,
    from_next,
    far_prev,
    far_next,
    even,
    odd,
    even_low,
    odd_low,
    q_near,
    q_far,
    wide,
    terms,
    back,
    vol_down,
    vol_up,
    back_prev,
    back_next,
    load_sem,
    ls,
    lr,
    index_sem,
    ns,
    nr,
    fs,
    fr,
    zs,
    zr,
    es,
    er,
    ps,
    pr,
    gs,
    gr,
    hs,
    hr,
    ws,
    wr,
    vs,
    vr,
):
    slab, me = lax.axis_index("slab"), lax.axis_index("angle")
    x, z = me // 2, lax.rem(me, 2)
    has_prev, has_next = slab > 0, slab < slabs - 1
    blocks, _, blk = vol_ref.shape
    width = dual_ref.shape[1]
    det = width // blk
    rows = det * 8
    seg = blk
    pairs = 8 * seg
    tile_count = tiles.shape[0]

    def group(k):
        return 2 * lax.rem(x + k % 4, 4) + (1 - z if k >= 4 else z)

    def device(k):
        return (slab, group(k))

    def mirror(k):
        return (4 - k % 4) % 4 + 4 * (k // 4)

    prev, following = (slab - 1, me), (slab + 1, me)
    far_me = 2 * x + 1 - z
    prev_far, following_far = (slab - 1, far_me), (slab + 1, far_me)

    barrier = pltpu.get_barrier_semaphore()
    for k in range(1, 8):
        pl.semaphore_signal(barrier, inc=1, device_id=device(k), device_id_type=MESH)

    @pl.when(has_prev)
    def _():
        pl.semaphore_signal(barrier, inc=1, device_id=prev, device_id_type=MESH)
        pl.semaphore_signal(barrier, inc=1, device_id=prev_far, device_id_type=MESH)

    @pl.when(has_next)
    def _():
        pl.semaphore_signal(barrier, inc=1, device_id=following, device_id_type=MESH)
        pl.semaphore_signal(barrier, inc=1, device_id=following_far, device_id_type=MESH)

    load_tiles = pltpu.make_async_copy(tiles_hbm, tiles, load_sem.at[0])
    load_ramp = pltpu.make_async_copy(ramp_hbm, ramp, load_sem.at[1])
    load_tiles.start()
    load_ramp.start()

    lane = lax.broadcasted_iota(jnp.int32, (1, seg), 1)
    for j in range(8):
        cols = pl.ds(j * seg, seg)
        out_lists[j, 0:1, :] = jnp.clip(lists_ref[0, :, cols] - j * blocks, 0, blocks - 1)
        out_lists[j, 1:2, :] = jnp.where(lane < live_ref[0, j], lists_ref[1, :, cols], det)
        out_lists[j, 2:3, :] = lists_ref[2, :, cols]
        out_lists[j, 3:8, :] = jnp.zeros((5, seg), jnp.int32)

    rounded[...] = vol_ref[...].reshape(blocks * 8, blk).astype(BF16)
    vol_down[...] = vol_ref[:, 7, :] * primal_w[0, 0]
    vol_up[...] = vol_ref[:, 0, :] * primal_w[0, 2]
    for k in range(8):
        wide[k * (det + 1) + det] = jnp.zeros((8, blk), F32)
    load_tiles.wait()

    def products(i, _):
        for u in range(0, 8, 2):
            t = i * 8 + u
            both = lax.dot_general(
                rounded[...], tiles[pl.ds(t, 2)].reshape(2 * blk, blk), CONTRACT_LAST, preferred_element_type=F32
            )
            dense[pl.ds(t * blocks, blocks)] = both[:, :blk].reshape(blocks, 8, blk)
            dense[pl.ds((t + 1) * blocks, blocks)] = both[:, blk:].reshape(blocks, 8, blk)
        return 0

    half = tile_count // 16
    lax.fori_loop(0, half, products, 0)
    present = 2 * (has_prev.astype(jnp.int32) + has_next.astype(jnp.int32))
    pl.semaphore_wait(barrier, 7 + present)

    list_copies = {}
    for k in (4, 6, 5, 7, 2, 1, 3):
        list_copies[k] = remote(
            out_lists.at[group(k)], in_lists.at[mirror(k)], ls.at[k - 1], lr.at[mirror(k) - 1], device(k)
        )
        list_copies[k].start()
    in_lists[0] = out_lists[me]
    lax.fori_loop(half, 2 * half, products, 0)

    row = lax.broadcasted_iota(jnp.int32, (1, 8, blk), 1)

    def volume_part(i, _):
        here = pl.ds(i * 8, 8)
        vol = vol_ref[here]
        before = jnp.where(row == 0, 0.0, pltpu.roll(primal_w[0, 0] * vol, 1, 1))
        after = jnp.where(row == 7, 0.0, pltpu.roll(primal_w[0, 2] * vol, 7, 1))
        new_vol[here] = vol + primal_w[0, 1] * vol + before + after
        return 0

    lax.fori_loop(0, blocks // 8, volume_part, 0)

    def split(value):
        high = value.astype(BF16)
        return high, (value - high.astype(F32)).astype(BF16)

    def to_index(k):
        copy = pltpu.make_async_copy(in_lists.at[k], index.at[k], index_sem.at[k])
        copy.start()
        return copy

    det_row = lax.broadcasted_iota(jnp.int32, (det, seg), 0)

    def project(k):
        def pick(j, _):
            for u in range(16):
                i = j * 16 + u
                picked[pl.ds(i, 8, stride=seg), :] = dense[index[k, 2, i] * blocks + index[k, 0, i]]
            return 0

        lax.fori_loop(0, seg // 16, pick, 0)
        parts = [split(picked[pl.ds(r * seg, seg)]) for r in range(8)]
        stacked = jnp.concatenate(
            [jnp.concatenate([p[0] for p in parts], axis=1), jnp.concatenate([p[1] for p in parts], axis=1)], axis=0
        )
        hot = jnp.where(det_row == in_lists[k, 1:2, :], 1.0, 0.0).astype(BF16)
        summed = jnp.dot(jnp.concatenate([hot, hot], axis=1), stacked, preferred_element_type=F32)
        for r in range(8):
            here = pl.ds(r * det, det)
            value = summed[:, r * blk : (r + 1) * blk]
            if k == 0:
                near[here] = value
            else:
                part[k - 1, here] = value.astype(BF16)

    near_copies, far_copies = [], []

    def send_part(k):
        d = k % 4
        if k < 4:
            copy = remote(part.at[k - 1], land_near.at[mirror(k) - 1], ns.at[d - 1], nr.at[mirror(d) - 1], device(d))
            near_copies.append(copy)
        else:
            copy = remote(part.at[k - 1], land_far.at[mirror(d) - 1], fs.at[d - 1], fr.at[mirror(d) - 1], device(d))
            far_copies.append(copy)
        copy.start()

    for k in (1, 3, 2):
        list_copies[k].wait_recv()
    moves = [to_index(k) for k in (0, 1, 3, 2)]
    for move in moves:
        move.wait()
    for k in (1, 3, 2):
        project(k)
        send_part(k)
    project(0)
    for k in (4, 5, 7, 6):
        list_copies[k].wait_recv()
    moves = [to_index(k) for k in (4, 5, 7, 6)]
    for move in moves:
        move.wait()
    for k in (6, 5, 7):
        project(k)
        send_part(k)
    project(4)

    for copy in far_copies:
        copy.wait_recv()
    total = part[3].astype(F32)
    for d in range(3):
        total = total + land_far[d].astype(F32)
    send_z[...] = total.astype(BF16)
    across = remote(send_z, land_z, zs.at[0], zr.at[0], device(4))
    across.start()
    first, last = pl.ds(0, det), pl.ds(rows - det, det)
    far_up = remote(send_z.at[first], far_next, ps.at[0], pr.at[0], prev_far)
    far_down = remote(send_z.at[last], far_prev, ps.at[1], pr.at[1], following_far)

    @pl.when(has_prev)
    def _():
        far_up.start()

    @pl.when(has_next)
    def _():
        far_down.start()

    for copy in near_copies:
        copy.wait_recv()
    whole = pl.ds(0, rows)
    total = near[whole]
    for d in range(3):
        total = total + land_near[d].astype(F32)
    near[whole] = total
    for b in range(det):
        cols = pl.ds(b * blk, blk)
        misfit[:, cols] = near[pl.ds(b, 8, stride=det), :] - meas_ref[:, cols]
    down[...] = dual_w[0, 0] * dual_ref[7:8, :] + dual_w[1, 0] * misfit[7:8, :]
    up[...] = dual_w[0, 2] * dual_ref[0:1, :] + dual_w[1, 2] * misfit[0:1, :]
    near_down = remote(down, from_prev, es.at[0], er.at[0], following)
    near_up = remote(up, from_next, es.at[1], er.at[1], prev)

    @pl.when(has_next)
    def _():
        near_down.start()

    @pl.when(has_prev)
    def _():
        near_up.start()

    @pl.when(has_prev)
    def _():
        near_down.wait_recv()
        far_down.wait_recv()

    @pl.when(jnp.logical_not(has_prev))
    def _():
        from_prev[...] = jnp.zeros_like(from_prev)
        far_prev[...] = jnp.zeros_like(far_prev)

    @pl.when(has_next)
    def _():
        near_up.wait_recv()
        far_up.wait_recv()

    @pl.when(jnp.logical_not(has_next))
    def _():
        from_next[...] = jnp.zeros_like(from_next)
        far_next[...] = jnp.zeros_like(far_next)

    load_ramp.wait()
    across.wait_recv()
    near[whole] = land_z[...].astype(F32)
    flat_row = lax.broadcasted_iota(jnp.int32, (8, blk), 0)
    before_far = far_prev[...].astype(F32) * dual_w[1, 0]
    after_far = far_next[...].astype(F32) * dual_w[1, 2]

    def updated(b):
        cols = pl.ds(b * blk, blk)
        dual = dual_ref[:, cols]
        mis = misfit[:, cols] + near[pl.ds(b, 8, stride=det), :]
        before = pltpu.roll(dual_w[0, 0] * dual + dual_w[1, 0] * mis, 1, 0)
        after = pltpu.roll(dual_w[0, 2] * dual + dual_w[1, 2] * mis, 7, 0)
        before = jnp.where(flat_row == 0, from_prev[:, cols] + before_far[b : b + 1], before)
        after = jnp.where(flat_row == 7, from_next[:, cols] + after_far[b : b + 1], after)
        new = dual + dual_w[0, 1] * dual + dual_w[1, 1] * mis + before + after
        new_dual[:, cols] = new
        return new

    news = [updated(b) for b in range(det)]
    for b in range(det):
        high, low = split(jnp.concatenate([news[b], news[(b + 1) % det]], axis=0))
        for base in (0, rows):
            if b % 2 == 0:
                even[pl.ds(base + b * 8, 16)] = high
                even_low[pl.ds(base + b * 8, 16)] = low
            else:
                odd[pl.ds(base + (b - 1) * 8, 16)] = high
                odd_low[pl.ds(base + (b - 1) * 8, 16)] = low
    total = jnp.zeros((rows, 2 * blk), F32)
    small = jnp.zeros((rows, blk), F32)
    for k in range(0, det, 2):
        here = pl.ds((det - k) * 8 % rows, rows)
        there = pl.ds((det - k - 2) * 8, rows)
        weight = ramp[pl.ds(k * blk, 2 * blk)]
        high = jnp.concatenate([even[here], odd[there]], axis=1)
        low = jnp.concatenate([even_low[here], odd_low[there]], axis=1)
        total = total + jnp.dot(high, weight, preferred_element_type=F32)
        small = small + jnp.dot(low, weight[:, :blk], preferred_element_type=F32)
    small = small + total[:, blk:] + total[:, :blk]
    for b in range(0, det, 2):
        both = jnp.concatenate([new_dual[:, pl.ds(b * blk, blk)], new_dual[:, pl.ds((b + 1) * blk, blk)]], axis=0)
        q_near[0, pl.ds(b * 8, 16)] = (0.5 * both + small[b * 8 : b * 8 + 16]).astype(BF16)

    over = remote(q_near.at[0], q_far.at[0], gs.at[0], gr.at[0], device(4))
    over.start()
    around = []
    for k in (2, 1, 3):
        copy = remote(q_near.at[0], q_near.at[mirror(k)], hs.at[k - 1], hr.at[mirror(k) - 1], device(k))
        copy.start()
        around.append(copy)

    def widen(k, value):
        wide[pl.ds(k * (det + 1), det)] = value.reshape(det, 8, blk).astype(F32)

    none = jnp.zeros((8, blk), F32)

    def back_products(lo, hi):
        def some(j, _):
            k = j // 2
            for u in range(0, 64, 2):
                sides = []
                for w in range(2):
                    i = lax.rem(j, 2) * 64 + u + w
                    value = wide[k * (det + 1) + index[k, 1, i]]
                    sides.append(jnp.concatenate([value, none] if w == 0 else [none, value], axis=0))
                i = lax.rem(j, 2) * 64 + u
                weight = jnp.concatenate([tiles[index[k, 2, i]], tiles[index[k, 2, i + 1]]], axis=0)
                left = jnp.concatenate(sides, axis=1).astype(BF16)
                both = jnp.dot(left, weight, preferred_element_type=F32)
                p = k * seg + i
                terms[pl.ds(p, 8, stride=pairs), :] = both[:8]
                terms[pl.ds(p + 1, 8, stride=pairs), :] = both[8:]
            return 0

        lax.fori_loop(2 * lo, 2 * hi, some, 0)

    vox_row = lax.broadcasted_iota(jnp.int32, (blocks, seg), 0)

    def hots(lo):
        hot = [jnp.where(vox_row == in_lists[k, 0:1, :], 1.0, 0.0).astype(BF16) for k in range(lo, lo + 4)]
        return jnp.concatenate(hot + hot, axis=1)

    def scattered(hot, lo, r):
        high, low = split(terms[pl.ds(r * pairs + lo * seg, 4 * seg)])
        return jnp.dot(hot, jnp.concatenate([high, low], axis=0), preferred_element_type=F32)

    widen(0, q_near[0])
    back_products(0, 1)
    for copy in around:
        copy.wait_recv()
    for k in range(1, 4):
        widen(k, q_near[k])
    back_products(1, 4)
    hot = hots(0)
    for r in range(8):
        back[pl.ds(r * blocks, blocks)] = scattered(hot, 0, r)

    over.wait_recv()
    onward = []
    for k in (2, 1, 3):
        copy = remote(q_far.at[0], q_far.at[mirror(k)], ws.at[k - 1], wr.at[mirror(k) - 1], device(k))
        copy.start()
        onward.append(copy)
    widen(4, q_far[0])
    back_products(4, 5)
    for copy in onward:
        copy.wait_recv()
    for k in range(1, 4):
        widen(4 + k, q_far[k])
    back_products(5, 8)
    hot = hots(4)

    def finish(r):
        back[pl.ds(r * blocks, blocks)] += scattered(hot, 4, r)

    finish(0)
    finish(7)
    vol_up[...] += primal_w[1, 2] * back[pl.ds(0, blocks)]
    vol_down[...] += primal_w[1, 0] * back[pl.ds(7 * blocks, blocks)]
    to_next = remote(vol_down, back_prev, vs.at[0], vr.at[0], following)
    to_prev = remote(vol_up, back_next, vs.at[1], vr.at[1], prev)

    @pl.when(has_next)
    def _():
        to_next.start()

    @pl.when(has_prev)
    def _():
        to_prev.start()

    for r in range(1, 7):
        finish(r)

    for r in range(8):
        value = primal_w[1, 1] * back[pl.ds(r * blocks, blocks)]
        if r > 0:
            value = value + primal_w[1, 0] * back[pl.ds((r - 1) * blocks, blocks)]
        if r < 7:
            value = value + primal_w[1, 2] * back[pl.ds((r + 1) * blocks, blocks)]
        terms[pl.ds(r * blocks, blocks)] = value

    @pl.when(has_prev)
    def _():
        to_next.wait_recv()
        terms[pl.ds(0, blocks)] += back_prev[...]

    @pl.when(has_next)
    def _():
        to_prev.wait_recv()
        terms[pl.ds(7 * blocks, blocks)] += back_next[...]

    def merge(i, _):
        for u in range(16):
            v = i * 16 + u
            new_vol[v] += terms[pl.ds(v, 8, stride=blocks), :]
        return 0

    lax.fori_loop(0, blocks // 16, merge, 0)

    for copy in list(list_copies.values()) + near_copies + far_copies + [across, over] + around + onward:
        copy.wait_send()

    @pl.when(has_prev)
    def _():
        far_up.wait_send()
        near_up.wait_send()
        to_prev.wait_send()

    @pl.when(has_next)
    def _():
        far_down.wait_send()
        near_down.wait_send()
        to_next.wait_send()


def on_device(volume, dual, measured, tiles, lists, live, dual_kernel, primal_kernel):
    groups, slabs = lax.axis_size("angle"), lax.axis_size("slab")
    blocks, _, blk = volume.shape
    width = dual.shape[2]
    det = width // blk
    rows = det * 8
    vmem, smem = pl.BlockSpec(memory_space=pltpu.VMEM), pl.BlockSpec(memory_space=pltpu.SMEM)
    hbm = pl.BlockSpec(memory_space=pl.ANY)
    dma = pltpu.SemaphoreType.DMA
    ramp = jnp.asarray(ramp_matrix(width, blk))
    new_volume, new_dual = pl.pallas_call(
        functools.partial(step_kernel, slabs),
        out_shape=[jax.ShapeDtypeStruct(volume.shape, F32), jax.ShapeDtypeStruct((8, width), F32)],
        in_specs=[vmem, smem, vmem, vmem, vmem, hbm, hbm, smem, smem],
        out_specs=[vmem, vmem],
        scratch_shapes=[
            pltpu.VMEM(tiles.shape, BF16),
            pltpu.VMEM(ramp.shape, BF16),
            pltpu.VMEM((tiles.shape[0] * blocks, 8, blk), F32),
            pltpu.VMEM((blocks * 8, blk), BF16),
            pltpu.VMEM((groups, 8, blk), jnp.int32),
            pltpu.VMEM((groups, 8, blk), jnp.int32),
            pltpu.SMEM((groups, 8, blk), jnp.int32),
            pltpu.VMEM((9 * blk, blk), F32),
            pltpu.VMEM((7, rows, blk), BF16),
            pltpu.VMEM((3, rows, blk), BF16),
            pltpu.VMEM((3, rows, blk), BF16),
            pltpu.VMEM((rows + det, blk), F32),
            pltpu.VMEM((rows, blk), BF16),
            pltpu.VMEM((rows, blk), BF16),
            pltpu.VMEM((8, width), F32),
        ]
        + [pltpu.VMEM((1, width), F32)] * 4
        + [pltpu.VMEM((det, blk), BF16)] * 2
        + [pltpu.VMEM((2 * rows, blk), BF16)] * 4
        + [pltpu.VMEM((4, rows, blk), BF16)] * 2
        + [
            pltpu.VMEM((groups * (det + 1), 8, blk), F32),
            pltpu.VMEM((9 * groups * blk, blk), F32),
            pltpu.VMEM((8 * blocks, blk), F32),
        ]
        + [pltpu.VMEM((blocks, blk), F32)] * 4
        + [dma((2,)), dma((7,)), dma((7,)), dma((8,))]
        + [dma((3,))] * 4
        + [dma((1,))] * 2
        + [dma((2,))] * 4
        + [dma((1,))] * 2
        + [dma((3,))] * 4
        + [dma((2,))] * 2,
        compiler_params=pltpu.CompilerParams(
            collective_id=0, has_side_effects=True, vmem_limit_bytes=VMEM_LIMIT
        ),
    )(lists, live, volume, dual[0], measured[0], tiles, ramp, dual_kernel, primal_kernel)
    return (new_volume, new_dual[None])


def solution(mesh):
    in_specs = (
        P("angle", "slab", None),
        P("angle", "slab", None),
        P("angle", "slab", None),
        P(),
        P(None, "slab", "angle"),
        P("slab", "angle"),
        P(),
        P(),
    )
    out_specs = (P("angle", "slab", None), P("angle", "slab", None))
    return jax.shard_map(
        on_device, mesh=mesh, in_specs=in_specs, out_specs=out_specs, check_vma=False
    )
```

time: 657 us -> 68.9 us (0.10)
  waiting for transfers between devices: 282 us -> 0 us
  local copies, waits for them, and re-layouts: 154 us -> 3.44 us
  matrix products: 88.1 us -> 0 us
  Pallas kernels: 0 us -> 64.6 us
  loops' own time: 59.8 us -> 0 us
  other arithmetic: 39.5 us -> 0 us
  starting transfers between devices: 13.8 us -> 0 us
  between operations: 14.3 us -> 0.64 us
    reduce_scatter x1 -> x0, waiting for transfers between devices: 164 us -> none  [on_device(): lax.psum_scatter(apply_blocks(q_blocks, det_ids, vox_ids, tile_ids, alive...]
    all_gather x1 -> x0, waiting for transfers between devices: 113 us -> none  [on_device(): lax.all_gather(volume.astype(jnp.bfloat16), 'angle', axis=0, tiled=True)]
    dot_general x108 -> x0, matrix products: 88.1 us -> none  [the longest x32 56.8 us: one_block(): jnp.einsum(formula, taken, tile_set, preferred_element_type=jnp.float32)]
    gather x32 -> x0, local copies, waits for them, and re-layouts: 75.2 us -> none  [one_block(): tile_set = jnp.take(tiles, tile_pick, axis=0)]
    pallas_call x0 -> x1, Pallas kernels: none -> 64.6 us  [on_device(): pl.pallas_call(functools.partial(step_kernel, slabs), out_shape=[jax.Shap...]
    another operation x2 -> x0, loops' own time: 59.8 us -> none  [apply_blocks(): return lax.fori_loop(0, entry_total // block_len, one_block, start_acc)]
    dynamic_slice x128 -> x0, local copies, waits for them, and re-layouts: 56.5 us -> none  [the longest x16 17.3 us: one_block(): current = lax.dynamic_slice_in_dim(accum, put_base, put_span, 0)]
    sub x32 -> x0, other arithmetic: 21.8 us -> none  [the longest x16 11.6 us: one_block(): picks = lax.dynamic_slice_in_dim(pick_idx, begin_at, block_len) - pick_base]
  transfers between devices with their start and end apart: 6 -> 0, of which waited for: 4 -> 0; matrix products, arithmetic and copies ran while one was open for 1% -> 0% of each run, Pallas kernels for 0% -> 0%
where the time goes in v2:
time: 68.9 us; the launch traced here: 68.7 us
  Pallas kernels  64.6 us (94%)
  local copies, waits for them, and re-layouts  3.44 us (5%)
    pallas_call x1, Pallas kernels, on_device(): pl.pallas_call(functools.partial(step_kernel, slabs), out_shape=[jax.Shap...  64.6 us
    unnamed x2, local copies, waits for them, and re-layouts  3.44 us

profile of v2, /device:TPU:1, one launch (start us, length us, event | category | flops | bytes accessed | tf_op | source)
XLA Modules:
  0.0 68.7 jit_solution(11753678278705028592)
XLA Ops:
  0.6 64.6 %shard_map.104 = (f32[128,8,128]{2,1,0:T(8,128)}, f32[8,4096]{1,0:T(8,128)}) custom-call(s32[3,1,1024]{2,1,0:T(1,128)} %lists_ref.1, s32[1,8]{1,0:T(1,128)} %live_ref.1, f32[128,8,128]{2,1,0:T(8,128)} %vol_ref.1, f32[8,4096]{1,0:T(8,128)} %bitcast.3, f32[8,4096]{1,0:T(8,128)} %bitcast.4, bf16[64,128,128]{2,1,0:T(8,128)(2,1)} %tiles_hbm.1, ...), custom_call_target="tpu_custom_call" | custom-call | tf_op jit(solution)/shard_map/pallas_call | solution.py:518
  65.3 1.9 %copy.13 = f32[128,8,128]{2,1,0:T(8,128)} copy(f32[128,8,128]{2,1,0:T(8,128)} %get-tuple-element.8) | data formatting | bytes 1048576
  67.1 1.6 %copy.14 = f32[1,8,4096]{2,1,0:T(8,128)} copy(f32[1,8,4096]{2,1,0:T(8,128)} %bitcast.5) | data formatting | bytes 262144

commit v3 on v2

--- a/solution.py
+++ b/solution.py
@@ -42,21 +42,25 @@
     slabs,
     lists_ref,
     live_ref,
-    vol_ref,
-    dual_ref,
-    meas_ref,
+    vol_hbm,
+    dual_hbm,
+    meas_hbm,
     tiles_hbm,
     ramp_hbm,
     dual_w,
     primal_w,
     new_vol,
     new_dual,
+    vol_ref,
+    dual_ref,
+    meas_ref,
     tiles,
     ramp,
     dense,
     rounded,
     out_lists,
     in_lists,
+    prepared,
     index,
     picked,
     part,
@@ -146,10 +150,14 @@
         pl.semaphore_signal(barrier, inc=1, device_id=following, device_id_type=MESH)
         pl.semaphore_signal(barrier, inc=1, device_id=following_far, device_id_type=MESH)
 
-    load_tiles = pltpu.make_async_copy(tiles_hbm, tiles, load_sem.at[0])
-    load_ramp = pltpu.make_async_copy(ramp_hbm, ramp, load_sem.at[1])
-    load_tiles.start()
-    load_ramp.start()
+    loads = [
+        pltpu.make_async_copy(source, target, load_sem.at[i])
+        for i, (source, target) in enumerate(
+            [(tiles_hbm, tiles), (vol_hbm, vol_ref), (dual_hbm, dual_ref), (meas_hbm, meas_ref), (ramp_hbm, ramp)]
+        )
+    ]
+    for load in loads:
+        load.start()
 
     lane = lax.broadcasted_iota(jnp.int32, (1, seg), 1)
     for j in range(8):
@@ -159,12 +167,20 @@
         out_lists[j, 2:3, :] = lists_ref[2, :, cols]
         out_lists[j, 3:8, :] = jnp.zeros((5, seg), jnp.int32)
 
+    def prepare(k):
+        voxel, detector, tile = in_lists[k, 0:1, :], in_lists[k, 1:2, :], in_lists[k, 2:3, :]
+        prepared[k, 0:1, :] = tile * blocks + voxel
+        prepared[k, 1:2, :] = detector + k * (det + 1)
+        prepared[k, 2:8, :] = in_lists[k, 2:8, :]
+        copy = pltpu.make_async_copy(prepared.at[k], index.at[k], index_sem.at[k])
+        copy.start()
+        return copy
+
+    in_lists[0] = out_lists[me]
+    own_index = prepare(0)
+    loads[0].wait()
+    loads[1].wait()
     rounded[...] = vol_ref[...].reshape(blocks * 8, blk).astype(BF16)
-    vol_down[...] = vol_ref[:, 7, :] * primal_w[0, 0]
-    vol_up[...] = vol_ref[:, 0, :] * primal_w[0, 2]
-    for k in range(8):
-        wide[k * (det + 1) + det] = jnp.zeros((8, blk), F32)
-    load_tiles.wait()
 
     def products(i, _):
         for u in range(0, 8, 2):
@@ -176,99 +192,110 @@
             dense[pl.ds((t + 1) * blocks, blocks)] = both[:, blk:].reshape(blocks, 8, blk)
         return 0
 
-    half = tile_count // 16
-    lax.fori_loop(0, half, products, 0)
+    early = tile_count // 8 - 2
+    lax.fori_loop(0, early, products, 0)
     present = 2 * (has_prev.astype(jnp.int32) + has_next.astype(jnp.int32))
     pl.semaphore_wait(barrier, 7 + present)
 
     list_copies = {}
-    for k in (4, 6, 5, 7, 2, 1, 3):
+    for k in (6, 5, 7, 4, 2, 1, 3):
         list_copies[k] = remote(
             out_lists.at[group(k)], in_lists.at[mirror(k)], ls.at[k - 1], lr.at[mirror(k) - 1], device(k)
         )
         list_copies[k].start()
-    in_lists[0] = out_lists[me]
-    lax.fori_loop(half, 2 * half, products, 0)
-
-    row = lax.broadcasted_iota(jnp.int32, (1, 8, blk), 1)
-
-    def volume_part(i, _):
-        here = pl.ds(i * 8, 8)
-        vol = vol_ref[here]
-        before = jnp.where(row == 0, 0.0, pltpu.roll(primal_w[0, 0] * vol, 1, 1))
-        after = jnp.where(row == 7, 0.0, pltpu.roll(primal_w[0, 2] * vol, 7, 1))
-        new_vol[here] = vol + primal_w[0, 1] * vol + before + after
-        return 0
-
-    lax.fori_loop(0, blocks // 8, volume_part, 0)
+    lax.fori_loop(early, tile_count // 8, products, 0)
 
     def split(value):
         high = value.astype(BF16)
         return high, (value - high.astype(F32)).astype(BF16)
 
-    def to_index(k):
-        copy = pltpu.make_async_copy(in_lists.at[k], index.at[k], index_sem.at[k])
-        copy.start()
-        return copy
-
     det_row = lax.broadcasted_iota(jnp.int32, (det, seg), 0)
 
     def project(k):
         def pick(j, _):
-            for u in range(16):
-                i = j * 16 + u
-                picked[pl.ds(i, 8, stride=seg), :] = dense[index[k, 2, i] * blocks + index[k, 0, i]]
+            for u in range(32):
+                i = j * 32 + u
+                picked[pl.ds(i, 8, stride=seg + 8), :] = dense[index[k, 0, i]]
             return 0
 
-        lax.fori_loop(0, seg // 16, pick, 0)
-        parts = [split(picked[pl.ds(r * seg, seg)]) for r in range(8)]
+        lax.fori_loop(0, seg // 32, pick, 0)
+        parts = [split(picked[pl.ds(r * (seg + 8), seg)]) for r in range(8)]
         stacked = jnp.concatenate(
             [jnp.concatenate([p[0] for p in parts], axis=1), jnp.concatenate([p[1] for p in parts], axis=1)], axis=0
         )
         hot = jnp.where(det_row == in_lists[k, 1:2, :], 1.0, 0.0).astype(BF16)
-        summed = jnp.dot(jnp.concatenate([hot, hot], axis=1), stacked, preferred_element_type=F32)
+        return jnp.dot(jnp.concatenate([hot, hot], axis=1), stacked, preferred_element_type=F32)
+
+    def turn(j):
+        return lax.rem(j * (j + 1) // 2, 4)
+
+    near_copies = {
+        d: remote(part.at[d], land_near.at[mirror(d) - 1], ns.at[d - 1], nr.at[mirror(d) - 1], device(d))
+        for d in (1, 3, 2)
+    }
+    far_copies = {
+        d: remote(part.at[d + 4], land_far.at[mirror(d) - 1], fs.at[d - 1], fr.at[mirror(d) - 1], device(d))
+        for d in (2, 3, 1)
+    }
+
+    def at_step(j, step):
+        return pl.when(j == step)
+
+    def receive(ks):
+        for k in ks:
+            list_copies[k].wait_recv()
+        copies = [prepare(k) for k in ks]
+        for copy in copies:
+            copy.wait()
+
+    def near_part(j, _):
+        k = turn(j)
+
+        @at_step(j, 1)
+        def _():
+            receive((1, 3, 2))
+
+        summed = project(k)
         for r in range(8):
             here = pl.ds(r * det, det)
-            value = summed[:, r * blk : (r + 1) * blk]
-            if k == 0:
-                near[here] = value
-            else:
-                part[k - 1, here] = value.astype(BF16)
-
-    near_copies, far_copies = [], []
-
-    def send_part(k):
-        d = k % 4
-        if k < 4:
-            copy = remote(part.at[k - 1], land_near.at[mirror(k) - 1], ns.at[d - 1], nr.at[mirror(d) - 1], device(d))
-            near_copies.append(copy)
-        else:
-            copy = remote(part.at[k - 1], land_far.at[mirror(d) - 1], fs.at[d - 1], fr.at[mirror(d) - 1], device(d))
-            far_copies.append(copy)
-        copy.start()
-
-    for k in (1, 3, 2):
-        list_copies[k].wait_recv()
-    moves = [to_index(k) for k in (0, 1, 3, 2)]
-    for move in moves:
-        move.wait()
-    for k in (1, 3, 2):
-        project(k)
-        send_part(k)
-    project(0)
-    for k in (4, 5, 7, 6):
-        list_copies[k].wait_recv()
-    moves = [to_index(k) for k in (4, 5, 7, 6)]
-    for move in moves:
-        move.wait()
-    for k in (6, 5, 7):
-        project(k)
-        send_part(k)
-    project(4)
-
-    for copy in far_copies:
+            part[k, here] = summed[:, r * blk : (r + 1) * blk].astype(BF16)
+
+        @at_step(j, 0)
+        def _():
+            for r in range(8):
+                near[pl.ds(r * det, det)] = summed[:, r * blk : (r + 1) * blk]
+
+        for step, d in ((1, 1), (2, 3), (3, 2)):
+
+            @at_step(j, step)
+            def _():
+                near_copies[d].start()
+
+        return 0
+
+    def far_part(j, _):
+        k = 4 + turn(3 - j)
+        summed = project(k)
+        for r in range(8):
+            here = pl.ds(r * det, det)
+            part[k, here] = summed[:, r * blk : (r + 1) * blk].astype(BF16)
+
+        for step, d in ((0, 2), (1, 3), (2, 1)):
+
+            @at_step(j, step)
+            def _():
+                far_copies[d].start()
+
+        return 0
+
+    own_index.wait()
+    lax.fori_loop(0, 4, near_part, 0)
+    receive((4, 5, 7, 6))
+    lax.fori_loop(0, 4, far_part, 0)
+
+    for copy in far_copies.values():
         copy.wait_recv()
-    total = part[3].astype(F32)
+    total = part[4].astype(F32)
     for d in range(3):
         total = total + land_far[d].astype(F32)
     send_z[...] = total.astype(BF16)
@@ -286,7 +313,9 @@
     def _():
         far_down.start()
 
-    for copy in near_copies:
+    loads[2].wait()
+    loads[3].wait()
+    for copy in near_copies.values():
         copy.wait_recv()
     whole = pl.ds(0, rows)
     total = near[whole]
@@ -309,6 +338,23 @@
     def _():
         near_up.start()
 
+    vol_down[...] = vol_ref[:, 7, :] * primal_w[0, 0]
+    vol_up[...] = vol_ref[:, 0, :] * primal_w[0, 2]
+    for k in range(8):
+        wide[k * (det + 1) + det] = jnp.zeros((8, blk), F32)
+    row = lax.broadcasted_iota(jnp.int32, (1, 8, blk), 1)
+
+    def volume_part(i, _):
+        here = pl.ds(i * 8, 8)
+        vol = vol_ref[here]
+        before = jnp.where(row == 0, 0.0, pltpu.roll(primal_w[0, 0] * vol, 1, 1))
+        after = jnp.where(row == 7, 0.0, pltpu.roll(primal_w[0, 2] * vol, 7, 1))
+        new_vol[here] = vol + primal_w[0, 1] * vol + before + after
+        return 0
+
+    lax.fori_loop(0, blocks // 8, volume_part, 0)
+    loads[4].wait()
+
     @pl.when(has_prev)
     def _():
         near_down.wait_recv()
@@ -329,7 +375,6 @@
         from_next[...] = jnp.zeros_like(from_next)
         far_next[...] = jnp.zeros_like(far_next)
 
-    load_ramp.wait()
     across.wait_recv()
     near[whole] = land_z[...].astype(F32)
     flat_row = lax.broadcasted_iota(jnp.int32, (8, blk), 0)
@@ -375,71 +420,79 @@
 
     over = remote(q_near.at[0], q_far.at[0], gs.at[0], gr.at[0], device(4))
     over.start()
-    around = []
+    around, onward = {}, {}
     for k in (2, 1, 3):
-        copy = remote(q_near.at[0], q_near.at[mirror(k)], hs.at[k - 1], hr.at[mirror(k) - 1], device(k))
-        copy.start()
-        around.append(copy)
+        around[k] = remote(q_near.at[0], q_near.at[mirror(k)], hs.at[k - 1], hr.at[mirror(k) - 1], device(k))
+        around[k].start()
+        onward[k] = remote(q_far.at[0], q_far.at[mirror(k)], ws.at[k - 1], wr.at[mirror(k) - 1], device(k))
 
     def widen(k, value):
         wide[pl.ds(k * (det + 1), det)] = value.reshape(det, 8, blk).astype(F32)
 
-    none = jnp.zeros((8, blk), F32)
-
-    def back_products(lo, hi):
-        def some(j, _):
-            k = j // 2
-            for u in range(0, 64, 2):
-                sides = []
-                for w in range(2):
-                    i = lax.rem(j, 2) * 64 + u + w
-                    value = wide[k * (det + 1) + index[k, 1, i]]
-                    sides.append(jnp.concatenate([value, none] if w == 0 else [none, value], axis=0))
-                i = lax.rem(j, 2) * 64 + u
-                weight = jnp.concatenate([tiles[index[k, 2, i]], tiles[index[k, 2, i + 1]]], axis=0)
-                left = jnp.concatenate(sides, axis=1).astype(BF16)
-                both = jnp.dot(left, weight, preferred_element_type=F32)
-                p = k * seg + i
-                terms[pl.ds(p, 8, stride=pairs), :] = both[:8]
-                terms[pl.ds(p + 1, 8, stride=pairs), :] = both[8:]
-            return 0
-
-        lax.fori_loop(2 * lo, 2 * hi, some, 0)
+    def back_products(k):
+        for i in range(0, seg, 2):
+            left = jnp.concatenate([wide[index[k, 1, i]], wide[index[k, 1, i + 1]]], axis=0).astype(BF16)
+            weight = jnp.concatenate([tiles[index[k, 2, i]], tiles[index[k, 2, i + 1]]], axis=1)
+            both = jnp.dot(left, weight, preferred_element_type=F32)
+            p = k * seg + i
+            terms[pl.ds(p, 8, stride=pairs + 8), :] = both[:8, :blk]
+            terms[pl.ds(p + 1, 8, stride=pairs + 8), :] = both[8:, blk:]
 
     vox_row = lax.broadcasted_iota(jnp.int32, (blocks, seg), 0)
+
+    def scattered(hot, lo, r):
+        high, low = split(terms[pl.ds(r * (pairs + 8) + lo * seg, 4 * seg)])
+        both = jnp.dot(hot, jnp.concatenate([high, low], axis=1), preferred_element_type=F32)
+        return both[:, :blk] + both[:, blk:]
 
     def hots(lo):
         hot = [jnp.where(vox_row == in_lists[k, 0:1, :], 1.0, 0.0).astype(BF16) for k in range(lo, lo + 4)]
-        return jnp.concatenate(hot + hot, axis=1)
-
-    def scattered(hot, lo, r):
-        high, low = split(terms[pl.ds(r * pairs + lo * seg, 4 * seg)])
-        return jnp.dot(hot, jnp.concatenate([high, low], axis=0), preferred_element_type=F32)
+        return jnp.concatenate(hot, axis=1)
 
     widen(0, q_near[0])
-    back_products(0, 1)
-    for copy in around:
-        copy.wait_recv()
-    for k in range(1, 4):
-        widen(k, q_near[k])
-    back_products(1, 4)
+
+    def near_back(j, _):
+        @at_step(j, 1)
+        def _():
+            around[1].wait_recv()
+            around[3].wait_recv()
+            widen(1, q_near[1])
+            widen(3, q_near[3])
+
+        @at_step(j, 3)
+        def _():
+            around[2].wait_recv()
+            widen(2, q_near[2])
+
+        back_products(turn(j))
+        return 0
+
+    lax.fori_loop(0, 4, near_back, 0)
+    over.wait_recv()
+    for k in (2, 1, 3):
+        onward[k].start()
+    widen(4, q_far[0])
     hot = hots(0)
     for r in range(8):
         back[pl.ds(r * blocks, blocks)] = scattered(hot, 0, r)
 
-    over.wait_recv()
-    onward = []
-    for k in (2, 1, 3):
-        copy = remote(q_far.at[0], q_far.at[mirror(k)], ws.at[k - 1], wr.at[mirror(k) - 1], device(k))
-        copy.start()
-        onward.append(copy)
-    widen(4, q_far[0])
-    back_products(4, 5)
-    for copy in onward:
-        copy.wait_recv()
-    for k in range(1, 4):
-        widen(4 + k, q_far[k])
-    back_products(5, 8)
+    def far_back(j, _):
+        @at_step(j, 1)
+        def _():
+            onward[1].wait_recv()
+            onward[3].wait_recv()
+            widen(5, q_far[1])
+            widen(7, q_far[3])
+
+        @at_step(j, 3)
+        def _():
+            onward[2].wait_recv()
+            widen(6, q_far[2])
+
+        back_products(4 + turn(j))
+        return 0
+
+    lax.fori_loop(0, 4, far_back, 0)
     hot = hots(4)
 
     def finish(r):
@@ -469,7 +522,7 @@
             value = value + primal_w[1, 0] * back[pl.ds((r - 1) * blocks, blocks)]
         if r < 7:
             value = value + primal_w[1, 2] * back[pl.ds((r + 1) * blocks, blocks)]
-        terms[pl.ds(r * blocks, blocks)] = value
+        terms[pl.ds(r * (blocks + 8), blocks)] = value
 
     @pl.when(has_prev)
     def _():
@@ -479,17 +532,18 @@
     @pl.when(has_next)
     def _():
         to_prev.wait_recv()
-        terms[pl.ds(7 * blocks, blocks)] += back_next[...]
+        terms[pl.ds(7 * (blocks + 8), blocks)] += back_next[...]
 
     def merge(i, _):
         for u in range(16):
             v = i * 16 + u
-            new_vol[v] += terms[pl.ds(v, 8, stride=blocks), :]
+            new_vol[v] += terms[pl.ds(v, 8, stride=blocks + 8), :]
         return 0
 
     lax.fori_loop(0, blocks // 16, merge, 0)
 
-    for copy in list(list_copies.values()) + near_copies + far_copies + [across, over] + around + onward:
+    sent = [list_copies, near_copies, far_copies, around, onward]
+    for copy in [copy for group_of in sent for copy in group_of.values()] + [across, over]:
         copy.wait_send()
 
     @pl.when(has_prev)
@@ -503,6 +557,17 @@
         far_down.wait_send()
         near_down.wait_send()
         to_next.wait_send()
+
+
+def store_kernel(vol_ref, dual_ref, vol_out, dual_out, sem):
+    copies = [
+        pltpu.make_async_copy(source, target, sem.at[i])
+        for i, (source, target) in enumerate([(vol_ref, vol_out), (dual_ref, dual_out)])
+    ]
+    for copy in copies:
+        copy.start()
+    for copy in copies:
+        copy.wait()
 
 
 def on_device(volume, dual, measured, tiles, lists, live, dual_kernel, primal_kernel):
@@ -515,21 +580,25 @@
     hbm = pl.BlockSpec(memory_space=pl.ANY)
     dma = pltpu.SemaphoreType.DMA
     ramp = jnp.asarray(ramp_matrix(width, blk))
-    new_volume, new_dual = pl.pallas_call(
+    outs = pl.pallas_call(
         functools.partial(step_kernel, slabs),
-        out_shape=[jax.ShapeDtypeStruct(volume.shape, F32), jax.ShapeDtypeStruct((8, width), F32)],
-        in_specs=[vmem, smem, vmem, vmem, vmem, hbm, hbm, smem, smem],
+        out_shape=[pltpu.VMEM(volume.shape, F32), pltpu.VMEM((8, width), F32)],
+        in_specs=[vmem, smem, hbm, hbm, hbm, hbm, hbm, smem, smem],
         out_specs=[vmem, vmem],
         scratch_shapes=[
+            pltpu.VMEM(volume.shape, F32),
+            pltpu.VMEM((8, width), F32),
+            pltpu.VMEM((8, width), F32),
             pltpu.VMEM(tiles.shape, BF16),
             pltpu.VMEM(ramp.shape, BF16),
             pltpu.VMEM((tiles.shape[0] * blocks, 8, blk), F32),
             pltpu.VMEM((blocks * 8, blk), BF16),
             pltpu.VMEM((groups, 8, blk), jnp.int32),
             pltpu.VMEM((groups, 8, blk), jnp.int32),
+            pltpu.VMEM((groups, 8, blk), jnp.int32),
             pltpu.SMEM((groups, 8, blk), jnp.int32),
-            pltpu.VMEM((9 * blk, blk), F32),
-            pltpu.VMEM((7, rows, blk), BF16),
+            pltpu.VMEM((10 * blk, blk), F32),
+            pltpu.VMEM((8, rows, blk), BF16),
             pltpu.VMEM((3, rows, blk), BF16),
             pltpu.VMEM((3, rows, blk), BF16),
             pltpu.VMEM((rows + det, blk), F32),
@@ -543,11 +612,11 @@
         + [pltpu.VMEM((4, rows, blk), BF16)] * 2
         + [
             pltpu.VMEM((groups * (det + 1), 8, blk), F32),
-            pltpu.VMEM((9 * groups * blk, blk), F32),
+            pltpu.VMEM((9 * (groups * blk + 8), blk), F32),
             pltpu.VMEM((8 * blocks, blk), F32),
         ]
         + [pltpu.VMEM((blocks, blk), F32)] * 4
-        + [dma((2,)), dma((7,)), dma((7,)), dma((8,))]
+        + [dma((5,)), dma((7,)), dma((7,)), dma((8,))]
         + [dma((3,))] * 4
         + [dma((1,))] * 2
         + [dma((2,))] * 4
@@ -558,6 +627,13 @@
             collective_id=0, has_side_effects=True, vmem_limit_bytes=VMEM_LIMIT
         ),
     )(lists, live, volume, dual[0], measured[0], tiles, ramp, dual_kernel, primal_kernel)
+    new_volume, new_dual = pl.pallas_call(
+        store_kernel,
+        out_shape=[jax.ShapeDtypeStruct(volume.shape, F32), jax.ShapeDtypeStruct((8, width), F32)],
+        in_specs=[vmem, vmem],
+        out_specs=[hbm, hbm],
+        scratch_shapes=[dma((2,))],
+    )(*[pltpu.with_memory_space_constraint(out, pltpu.VMEM) for out in outs])
     return (new_volume, new_dual[None])
 
 

time: 68.9 us -> 62 us (0.90); the launches traced: 68.7 us -> 61 us
  Pallas kernels: 64.6 us -> 60.4 us
  local copies, waits for them, and re-layouts: 3.44 us -> 0 us
    pallas_call x1 -> x2, Pallas kernels: 64.6 us -> 60.4 us  [the longest x1 59.5 us: on_device(): pl.pallas_call(functools.partial(step_kernel, slabs), out_shape=[pltpu.VM...]
    unnamed x2 -> x0, local copies, waits for them, and re-layouts: 3.44 us -> none
where the time goes in v3:
time: 62 us; the launch traced here: 61 us
  Pallas kernels  60.4 us (97%)
  between operations  0.64 us (1%)
    pallas_call x1, Pallas kernels, on_device(): pl.pallas_call(functools.partial(step_kernel, slabs), out_shape=[pltpu.VM...  59.5 us

profile of v3, /device:TPU:1, one launch (start us, length us, event | category | flops | bytes accessed | tf_op | source)
XLA Modules:
  0.0 61.0 jit_solution(9104918470245911360)
XLA Ops:
  0.6 59.5 %shard_map.104 = (f32[128,8,128]{2,1,0:T(8,128)S(1)}, f32[8,4096]{1,0:T(8,128)S(1)}) custom-call(s32[3,1,1024]{2,1,0:T(1,128)} %lists_ref.1, s32[1,8]{1,0:T(1,128)} %live_ref.1, f32[128,8,128]{2,1,0:T(8,128)} %vol_hbm.1, f32[8,4096]{1,0:T(8,128)} %bitcast.3, f32[8,4096]{1,0:T(8,128)} %bitcast.4, bf16[64,128,128]{2,1,0:T(8,128)(2,1)} %tiles_hbm.1, ...), custom_call_target="tpu_custom_call" | custom-call | tf_op jit(solution)/shard_map/pallas_call | solution.py:583
  60.2 0.8 %shard_map.105 = (f32[128,8,128]{2,1,0:T(8,128)}, f32[8,4096]{1,0:T(8,128)}) custom-call(f32[128,8,128]{2,1,0:T(8,128)S(1)} %get-tuple-element.6.vol_ref, f32[8,4096]{1,0:T(8,128)S(1)} %get-tuple-element.7.dual_ref), custom_call_target="tpu_custom_call" | custom-call | tf_op jit(solution)/shard_map/pallas_call | solution.py:630

commit v4 on v3

--- a/solution.py
+++ b/solution.py
@@ -63,6 +63,7 @@
     prepared,
     index,
     picked,
+    picked_too,
     part,
     land_near,
     land_far,
@@ -192,7 +193,7 @@
             dense[pl.ds((t + 1) * blocks, blocks)] = both[:, blk:].reshape(blocks, 8, blk)
         return 0
 
-    early = tile_count // 8 - 2
+    early = tile_count // 8 - 4
     lax.fori_loop(0, early, products, 0)
     present = 2 * (has_prev.astype(jnp.int32) + has_next.astype(jnp.int32))
     pl.semaphore_wait(barrier, 7 + present)
@@ -211,20 +212,30 @@
 
     det_row = lax.broadcasted_iota(jnp.int32, (det, seg), 0)
 
-    def project(k):
-        def pick(j, _):
-            for u in range(32):
-                i = j * 32 + u
-                picked[pl.ds(i, 8, stride=seg + 8), :] = dense[index[k, 0, i]]
-            return 0
-
-        lax.fori_loop(0, seg // 32, pick, 0)
-        parts = [split(picked[pl.ds(r * (seg + 8), seg)]) for r in range(8)]
+    sides = (picked, picked_too)
+
+    def project(k, side, after=None):
+        parts = []
+        for r in range(8):
+            if after is not None:
+                for i in range(r * seg // 8, (r + 1) * seg // 8):
+                    sides[1 - side][pl.ds(i, 8, stride=seg + 8), :] = dense[index[after, 0, i]]
+            if k is not None:
+                parts.append(split(sides[side][pl.ds(r * (seg + 8), seg)]))
+        if k is None:
+            return
         stacked = jnp.concatenate(
             [jnp.concatenate([p[0] for p in parts], axis=1), jnp.concatenate([p[1] for p in parts], axis=1)], axis=0
         )
         hot = jnp.where(det_row == in_lists[k, 1:2, :], 1.0, 0.0).astype(BF16)
-        return jnp.dot(jnp.concatenate([hot, hot], axis=1), stacked, preferred_element_type=F32)
+        summed = jnp.dot(jnp.concatenate([hot, hot], axis=1), stacked, preferred_element_type=F32)
+        for r in range(8):
+            here = pl.ds(r * det, det)
+            value = summed[:, r * blk : (r + 1) * blk]
+            if k == 0:
+                near[here] = value
+            else:
+                part[k, here] = value.astype(BF16)
 
     def turn(j):
         return lax.rem(j * (j + 1) // 2, 4)
@@ -248,50 +259,25 @@
         for copy in copies:
             copy.wait()
 
-    def near_part(j, _):
-        k = turn(j)
-
-        @at_step(j, 1)
-        def _():
-            receive((1, 3, 2))
-
-        summed = project(k)
-        for r in range(8):
-            here = pl.ds(r * det, det)
-            part[k, here] = summed[:, r * blk : (r + 1) * blk].astype(BF16)
-
-        @at_step(j, 0)
-        def _():
-            for r in range(8):
-                near[pl.ds(r * det, det)] = summed[:, r * blk : (r + 1) * blk]
-
-        for step, d in ((1, 1), (2, 3), (3, 2)):
-
-            @at_step(j, step)
-            def _():
-                near_copies[d].start()
-
-        return 0
-
-    def far_part(j, _):
-        k = 4 + turn(3 - j)
-        summed = project(k)
-        for r in range(8):
-            here = pl.ds(r * det, det)
-            part[k, here] = summed[:, r * blk : (r + 1) * blk].astype(BF16)
-
-        for step, d in ((0, 2), (1, 3), (2, 1)):
-
-            @at_step(j, step)
-            def _():
-                far_copies[d].start()
-
-        return 0
-
     own_index.wait()
-    lax.fori_loop(0, 4, near_part, 0)
+    project(None, 1, 0)
+    receive((1, 3, 2))
+    project(0, 0, 1)
+    project(1, 1, 3)
+    near_copies[1].start()
+    project(3, 0, 2)
+    near_copies[3].start()
+    project(2, 1)
+    near_copies[2].start()
     receive((4, 5, 7, 6))
-    lax.fori_loop(0, 4, far_part, 0)
+    project(None, 1, 6)
+    project(6, 0, 7)
+    far_copies[2].start()
+    project(7, 1, 5)
+    far_copies[3].start()
+    project(5, 0, 4)
+    far_copies[1].start()
+    project(4, 1)
 
     for copy in far_copies.values():
         copy.wait_recv()
@@ -418,13 +404,20 @@
         both = jnp.concatenate([new_dual[:, pl.ds(b * blk, blk)], new_dual[:, pl.ds((b + 1) * blk, blk)]], axis=0)
         q_near[0, pl.ds(b * 8, 16)] = (0.5 * both + small[b * 8 : b * 8 + 16]).astype(BF16)
 
-    over = remote(q_near.at[0], q_far.at[0], gs.at[0], gr.at[0], device(4))
-    over.start()
+    step = rows // 2
+    halves = [pl.ds(0, step), pl.ds(step, step)]
+    over = []
+    for c, half in enumerate(halves):
+        over.append(remote(q_near.at[0, half], q_far.at[0, half], gs.at[c], gr.at[c], device(4)))
+        over[c].start()
     around, onward = {}, {}
     for k in (2, 1, 3):
         around[k] = remote(q_near.at[0], q_near.at[mirror(k)], hs.at[k - 1], hr.at[mirror(k) - 1], device(k))
         around[k].start()
-        onward[k] = remote(q_far.at[0], q_far.at[mirror(k)], ws.at[k - 1], wr.at[mirror(k) - 1], device(k))
+        for c, half in enumerate(halves):
+            onward[k, c] = remote(
+                q_far.at[0, half], q_far.at[mirror(k), half], ws.at[k - 1, c], wr.at[mirror(k) - 1, c], device(k)
+            )
 
     def widen(k, value):
         wide[pl.ds(k * (det + 1), det)] = value.reshape(det, 8, blk).astype(F32)
@@ -468,9 +461,10 @@
         return 0
 
     lax.fori_loop(0, 4, near_back, 0)
-    over.wait_recv()
-    for k in (2, 1, 3):
-        onward[k].start()
+    for c in range(2):
+        over[c].wait_recv()
+        for k in (2, 1, 3):
+            onward[k, c].start()
     widen(4, q_far[0])
     hot = hots(0)
     for r in range(8):
@@ -479,14 +473,15 @@
     def far_back(j, _):
         @at_step(j, 1)
         def _():
-            onward[1].wait_recv()
-            onward[3].wait_recv()
+            for k, c in ((1, 0), (3, 0), (1, 1), (3, 1)):
+                onward[k, c].wait_recv()
             widen(5, q_far[1])
             widen(7, q_far[3])
 
         @at_step(j, 3)
         def _():
-            onward[2].wait_recv()
+            for c in range(2):
+                onward[2, c].wait_recv()
             widen(6, q_far[2])
 
         back_products(4 + turn(j))
@@ -543,7 +538,7 @@
     lax.fori_loop(0, blocks // 16, merge, 0)
 
     sent = [list_copies, near_copies, far_copies, around, onward]
-    for copy in [copy for group_of in sent for copy in group_of.values()] + [across, over]:
+    for copy in [copy for group_of in sent for copy in group_of.values()] + [across] + over:
         copy.wait_send()
 
     @pl.when(has_prev)
@@ -598,6 +593,7 @@
             pltpu.VMEM((groups, 8, blk), jnp.int32),
             pltpu.SMEM((groups, 8, blk), jnp.int32),
             pltpu.VMEM((10 * blk, blk), F32),
+            pltpu.VMEM((10 * blk, blk), F32),
             pltpu.VMEM((8, rows, blk), BF16),
             pltpu.VMEM((3, rows, blk), BF16),
             pltpu.VMEM((3, rows, blk), BF16),
@@ -619,9 +615,9 @@
         + [dma((5,)), dma((7,)), dma((7,)), dma((8,))]
         + [dma((3,))] * 4
         + [dma((1,))] * 2
-        + [dma((2,))] * 4
-        + [dma((1,))] * 2
-        + [dma((3,))] * 4
+        + [dma((2,))] * 6
+        + [dma((3,))] * 2
+        + [dma((3, 2))] * 2
         + [dma((2,))] * 2,
         compiler_params=pltpu.CompilerParams(
             collective_id=0, has_side_effects=True, vmem_limit_bytes=VMEM_LIMIT

time: 62 us -> 61.1 us (0.985)
  no operation moved by 1% of the time
where the time goes in v4:
time: 61.1 us; the launch traced here: 60.5 us
  Pallas kernels  59.9 us (98%)
  between operations  0.64 us (1%)
    pallas_call x1, Pallas kernels, on_device(): pl.pallas_call(functools.partial(step_kernel, slabs), out_shape=[pltpu.VM...  59.1 us

profile of v4, /device:TPU:1, one launch (start us, length us, event | category | flops | bytes accessed | tf_op | source)
XLA Modules:
  0.0 60.5 jit_solution(12386046771406965341)
XLA Ops:
  0.6 59.1 %shard_map.104 = (f32[128,8,128]{2,1,0:T(8,128)S(1)}, f32[8,4096]{1,0:T(8,128)S(1)}) custom-call(s32[3,1,1024]{2,1,0:T(1,128)} %lists_ref.1, s32[1,8]{1,0:T(1,128)} %live_ref.1, f32[128,8,128]{2,1,0:T(8,128)} %vol_hbm.1, f32[8,4096]{1,0:T(8,128)} %bitcast.3, f32[8,4096]{1,0:T(8,128)} %bitcast.4, bf16[64,128,128]{2,1,0:T(8,128)(2,1)} %tiles_hbm.1, ...), custom_call_target="tpu_custom_call" | custom-call | tf_op jit(solution)/shard_map/pallas_call | solution.py:578
  59.7 0.8 %shard_map.105 = (f32[128,8,128]{2,1,0:T(8,128)}, f32[8,4096]{1,0:T(8,128)}) custom-call(f32[128,8,128]{2,1,0:T(8,128)S(1)} %get-tuple-element.6.vol_ref, f32[8,4096]{1,0:T(8,128)S(1)} %get-tuple-element.7.dual_ref), custom_call_target="tpu_custom_call" | custom-call | tf_op jit(solution)/shard_map/pallas_call | solution.py:626

commit v5 on v4

--- a/solution.py
+++ b/solution.py
@@ -40,17 +40,21 @@
 
 def step_kernel(
     slabs,
-    lists_ref,
-    live_ref,
+    lists_hbm,
+    live_hbm,
     vol_hbm,
     dual_hbm,
     meas_hbm,
     tiles_hbm,
     ramp_hbm,
+    dual_w_hbm,
+    primal_w_hbm,
+    new_vol,
+    new_dual,
+    lists_ref,
+    live_ref,
     dual_w,
     primal_w,
-    new_vol,
-    new_dual,
     vol_ref,
     dual_ref,
     meas_ref,
@@ -90,6 +94,7 @@
     vol_up,
     back_prev,
     back_next,
+    small_sem,
     load_sem,
     ls,
     lr,
@@ -151,6 +156,14 @@
         pl.semaphore_signal(barrier, inc=1, device_id=following, device_id_type=MESH)
         pl.semaphore_signal(barrier, inc=1, device_id=following_far, device_id_type=MESH)
 
+    small = [
+        pltpu.make_async_copy(source, target, small_sem.at[i])
+        for i, (source, target) in enumerate(
+            [(lists_hbm, lists_ref), (live_hbm, live_ref), (dual_w_hbm, dual_w), (primal_w_hbm, primal_w)]
+        )
+    ]
+    for load in small:
+        load.start()
     loads = [
         pltpu.make_async_copy(source, target, load_sem.at[i])
         for i, (source, target) in enumerate(
@@ -160,6 +173,8 @@
     for load in loads:
         load.start()
 
+    for load in small:
+        load.wait()
     lane = lax.broadcasted_iota(jnp.int32, (1, seg), 1)
     for j in range(8):
         cols = pl.ds(j * seg, seg)
@@ -578,9 +593,13 @@
     outs = pl.pallas_call(
         functools.partial(step_kernel, slabs),
         out_shape=[pltpu.VMEM(volume.shape, F32), pltpu.VMEM((8, width), F32)],
-        in_specs=[vmem, smem, hbm, hbm, hbm, hbm, hbm, smem, smem],
+        in_specs=[hbm] * 9,
         out_specs=[vmem, vmem],
         scratch_shapes=[
+            pltpu.VMEM(lists.shape, jnp.int32),
+            pltpu.SMEM(live.shape, jnp.int32),
+            pltpu.SMEM(dual_kernel.shape, F32),
+            pltpu.SMEM(primal_kernel.shape, F32),
             pltpu.VMEM(volume.shape, F32),
             pltpu.VMEM((8, width), F32),
             pltpu.VMEM((8, width), F32),
@@ -612,7 +631,7 @@
             pltpu.VMEM((8 * blocks, blk), F32),
         ]
         + [pltpu.VMEM((blocks, blk), F32)] * 4
-        + [dma((5,)), dma((7,)), dma((7,)), dma((8,))]
+        + [dma((4,)), dma((5,)), dma((7,)), dma((7,)), dma((8,))]
         + [dma((3,))] * 4
         + [dma((1,))] * 2
         + [dma((2,))] * 6

time: 61.1 us -> 60.3 us (0.987)
  Pallas kernels: 59.9 us -> 59 us
    pallas_call x1, Pallas kernels: 59.1 us -> 58.1 us  [on_device(): pl.pallas_call(functools.partial(step_kernel, slabs), out_shape=[pltpu.VM...]
where the time goes in v5:
time: 60.3 us; the launch traced here: 59.6 us
  Pallas kernels  59 us (98%)
  between operations  0.64 us (1%)
    pallas_call x1, Pallas kernels, on_device(): pl.pallas_call(functools.partial(step_kernel, slabs), out_shape=[pltpu.VM...  58.1 us

profile of v5, /device:TPU:1, one launch (start us, length us, event | category | flops | bytes accessed | tf_op | source)
XLA Modules:
  0.0 59.6 jit_solution(17855749993486266007)
XLA Ops:
  0.6 58.1 %shard_map.104 = (f32[128,8,128]{2,1,0:T(8,128)S(1)}, f32[8,4096]{1,0:T(8,128)S(1)}) custom-call(s32[3,1,1024]{2,1,0:T(1,128)} %lists_hbm.1, s32[1,8]{1,0:T(1,128)} %live_hbm.1, f32[128,8,128]{2,1,0:T(8,128)} %vol_hbm.1, f32[8,4096]{1,0:T(8,128)} %bitcast.3, f32[8,4096]{1,0:T(8,128)} %bitcast.4, bf16[64,128,128]{2,1,0:T(8,128)(2,1)} %tiles_hbm.1, ...), custom_call_target="tpu_custom_call" | custom-call | tf_op jit(solution)/shard_map/pallas_call | solution.py:593
  58.8 0.8 %shard_map.105 = (f32[128,8,128]{2,1,0:T(8,128)}, f32[8,4096]{1,0:T(8,128)}) custom-call(f32[128,8,128]{2,1,0:T(8,128)S(1)} %get-tuple-element.6.vol_ref, f32[8,4096]{1,0:T(8,128)S(1)} %get-tuple-element.7.dual_ref), custom_call_target="tpu_custom_call" | custom-call | tf_op jit(solution)/shard_map/pallas_call | solution.py:645

commit v6 on v5

--- a/solution.py
+++ b/solution.py
@@ -478,7 +478,7 @@
     lax.fori_loop(0, 4, near_back, 0)
     for c in range(2):
         over[c].wait_recv()
-        for k in (2, 1, 3):
+        for k in (1, 3, 2):
             onward[k, c].start()
     widen(4, q_far[0])
     hot = hots(0)

time: 60.3 us -> 60 us (level)
  no operation moved by 1% of the time
where the time goes in v6:
time: 60 us; the launch traced here: 59.8 us
  Pallas kernels  59.2 us (99%)
  between operations  0.64 us (1%)
    pallas_call x1, Pallas kernels, on_device(): pl.pallas_call(functools.partial(step_kernel, slabs), out_shape=[pltpu.VM...  58.4 us

profile of v6, /device:TPU:1, one launch (start us, length us, event | category | flops | bytes accessed | tf_op | source)
XLA Modules:
  0.0 59.8 jit_solution(4006152503684700101)
XLA Ops:
  0.6 58.4 %shard_map.104 = (f32[128,8,128]{2,1,0:T(8,128)S(1)}, f32[8,4096]{1,0:T(8,128)S(1)}) custom-call(s32[3,1,1024]{2,1,0:T(1,128)} %lists_hbm.1, s32[1,8]{1,0:T(1,128)} %live_hbm.1, f32[128,8,128]{2,1,0:T(8,128)} %vol_hbm.1, f32[8,4096]{1,0:T(8,128)} %bitcast.3, f32[8,4096]{1,0:T(8,128)} %bitcast.4, bf16[64,128,128]{2,1,0:T(8,128)(2,1)} %tiles_hbm.1, ...), custom_call_target="tpu_custom_call" | custom-call | tf_op jit(solution)/shard_map/pallas_call | solution.py:593
  59.0 0.8 %shard_map.105 = (f32[128,8,128]{2,1,0:T(8,128)}, f32[8,4096]{1,0:T(8,128)}) custom-call(f32[128,8,128]{2,1,0:T(8,128)S(1)} %get-tuple-element.6.vol_ref, f32[8,4096]{1,0:T(8,128)S(1)} %get-tuple-element.7.dual_ref), custom_call_target="tpu_custom_call" | custom-call | tf_op jit(solution)/shard_map/pallas_call | solution.py:645
